TPU v7x, 32 devices: a whole 2x2x4 slice. The times are simulated.
32 devices in a mesh: grp: 4 (over y, x), row: 8 (over z, core).
Axes of the slice: x: 2, y: 2, z: 4, core: 2. Of those that a mesh axis runs over, the one named last changes fastest.
Arguments:
- colatitude: float32 [65536], P(('grp', 'row')), may hold values from 0.05 to 3.09
- longitude: float32 [65536], P(('grp', 'row')), may hold values from -3.140625 to 3.140625
- observed: bfloat16 [2, 65536], P(None, ('grp', 'row')), may hold values from -6 to 6
- filter_taps: bfloat16 [2, 256], replicated, may hold values from -0.375 to 0.375
- segment_start: int32 [65536], P(('grp', 'row')), may hold values 0 or 1
- harmonic: int32 [2, 512], replicated, may hold values from -280 to 280, as said below
Outputs:
- normal: float32 [512, 512], P('row', 'grp')
- right_side: float32 [512], replicated
- diagonal: float32 [512], replicated
Inputs may be any that keep to these rules, and one draw needn't show every extreme that they name: `harmonic`: row 0 holds degrees from 2 to 280; row 1 holds orders whose magnitude is at most the column's degree; no two columns name the same pair; the pairs (280, 280) and (280, -280) are always present.
All inputs are finite; a program needn't handle non-finite values. No bound on the sum of `segment_start` on one device may be relied on, other than what follows from the above.
Results may differ from a plain program's by a relative error of at most 0.0041.
Values may be sent and summed in bfloat16 or wider, within the bound.
A program may use at most 64 MiB of HBM per device.

v0:
```python
import math

import jax
import jax.numpy as jnp
from jax import lax
from jax.sharding import PartitionSpec as P


def passed_along(array, axis, by):
    length = lax.axis_size(axis)
    pairs = [(i, i + by) for i in range(length) if 0 <= i + by < length]
    return lax.ppermute(array, axis, pairs)


def design_rows(colatitude, longitude, harmonic):
    degree = harmonic[0].astype(jnp.float32)
    order_index = harmonic[1]
    polar_angle = colatitude[:, None] * degree[None, :]
    azimuth = longitude[:, None] * jnp.abs(order_index).astype(jnp.float32)[None, :]
    azimuth_wave = jnp.where(order_index[None, :] >= 0, jnp.cos(azimuth), jnp.sin(azimuth))
    radial = (jnp.cos(polar_angle) * azimuth_wave).astype(jnp.bfloat16)
    along = (jnp.sin(polar_angle) * azimuth_wave).astype(jnp.bfloat16)
    return (radial, along)


def on_device(colatitude, longitude, observed, filter_taps, segment_start, harmonic):
    rows_here = colatitude.shape[0]
    tap_count = filter_taps.shape[1]
    halo_rows = tap_count - 1
    panel_width = harmonic.shape[1]
    radial, along = design_rows(colatitude, longitude, harmonic)
    running = jnp.cumsum(segment_start)
    keep_tail = running[rows_here - halo_rows :] == running[rows_here - 1]
    keep_mask = keep_tail.astype(jnp.bfloat16)
    sent_rows = (
        radial[rows_here - halo_rows :] * keep_mask[:, None],
        along[rows_here - halo_rows :] * keep_mask[:, None],
        observed[:, rows_here - halo_rows :] * keep_mask[None, :],
    )
    halo_radial, halo_along, halo_signal = passed_along(
        (sent_rows[0], sent_rows[1], sent_rows[2]), "row", 1
    )
    labels = jnp.concatenate([jnp.zeros((halo_rows,), jnp.int32), running])
    windows = (
        jnp.concatenate([halo_radial, radial], axis=0),
        jnp.concatenate([halo_along, along], axis=0),
    )
    signal_window = jnp.concatenate([halo_signal, observed], axis=1)
    filtered = []
    filtered_signal = []
    for component in range(2):
        reversed_taps = filter_taps[component, ::-1]
        tap_seed = jnp.concatenate([reversed_taps, jnp.zeros((tap_count,), filter_taps.dtype)])
        tap_table = jnp.tile(tap_seed, tap_count)[: tap_count * (2 * tap_count - 1)].reshape(
            tap_count, 2 * tap_count - 1
        )
        pieces = []
        signal_pieces = []
        for block_index in range(rows_here // tap_count):
            block_low = block_index * tap_count
            in_label = labels[block_low : block_low + 2 * tap_count - 1]
            out_label = labels[block_low + halo_rows : block_low + halo_rows + tap_count]
            valid_mask = out_label[:, None] == in_label[None, :]
            matrix = jnp.where(valid_mask, tap_table, jnp.zeros((), tap_table.dtype))
            pieces.append(
                jnp.dot(
                    matrix,
                    windows[component][block_low : block_low + 2 * tap_count - 1],
                    preferred_element_type=jnp.float32,
                ).astype(jnp.bfloat16)
            )
            signal_pieces.append(
                jnp.dot(
                    matrix,
                    signal_window[component, block_low : block_low + 2 * tap_count - 1],
                    preferred_element_type=jnp.float32,
                ).astype(jnp.bfloat16)
            )
        filtered.append(jnp.concatenate(pieces, axis=0))
        filtered_signal.append(jnp.concatenate(signal_pieces, axis=0))
    rows_total = rows_here * lax.axis_size("grp") * lax.axis_size("row")
    row_scale = 1.0 / rows_total
    gram_scale = 1.0 / math.sqrt(rows_total)
    gram_sum = jnp.zeros(
        (lax.axis_size("row") * (panel_width // lax.axis_size("row")), panel_width), jnp.float32
    )
    for filtered_field in filtered:
        gram_sum = gram_sum + lax.dot_general(
            filtered_field,
            filtered_field,
            (((0,), (0,)), ((), ())),
            preferred_element_type=jnp.float32,
        )
    owned_tile = lax.psum_scatter(gram_sum * gram_scale, "row", scatter_dimension=0, tiled=True)
    normal = lax.psum_scatter(owned_tile, "grp", scatter_dimension=1, tiled=True)
    tile_rows = normal.shape[0]
    tile_cols = normal.shape[1]
    row_labels = lax.axis_index("row") * tile_rows + jnp.arange(tile_rows, dtype=jnp.int32)
    col_labels = lax.axis_index("grp") * tile_cols + jnp.arange(tile_cols, dtype=jnp.int32)
    normal = jnp.where(
        row_labels[:, None] == col_labels[None, :], jnp.zeros((), jnp.float32), normal
    )
    rhs_term = jnp.dot(filtered_signal[0], filtered[0], preferred_element_type=jnp.float32)
    rhs_term = rhs_term + jnp.dot(
        filtered_signal[1], filtered[1], preferred_element_type=jnp.float32
    )
    square_term = jnp.sum(jnp.square(filtered[0].astype(jnp.float32)), axis=0)
    square_term = square_term + jnp.sum(jnp.square(filtered[1].astype(jnp.float32)), axis=0)
    right_side, diagonal = lax.psum(
        (rhs_term * gram_scale, square_term * row_scale), ("grp", "row")
    )
    return (normal, right_side, diagonal)


def solution(mesh):
    placed = (
        P(("grp", "row")),
        P(("grp", "row")),
        P(None, ("grp", "row")),
        P(),
        P(("grp", "row")),
        P(),
    )
    return jax.shard_map(
        on_device,
        mesh=mesh,
        in_specs=placed,
        out_specs=(P("row", "grp"), P(), P()),
        check_vma=False,
    )
```

profile of v0, /device:TPU:0, one launch (start us, length us, event | category | flops | bytes accessed | tf_op | source)
XLA Modules:
  0.0 175.5 jit_solution(1730183440685028859)
XLA Ops:
  7.2 1.0 reduce-window.9
  8.5 0.6 slice.275
  9.1 0.7 compare_convert_fusion
  9.8 1.3 slice_multiply_fusion.2
  11.1 2.9 %collective-permute-start.2 = (bf16[2,255]{1,0:T(2,128)(2,1)}, bf16[2,255]{1,0:T(2,128)(2,1)}, u32[]{:S(2)}, u32[]{:S(2)}) collective-permute-start(bf16[2,255]{1,0:T(2,128)(2,1)} %slice_multiply_fusion.2), channel_id=1, source_target_pairs={{0,1},{1,2},{2,3},{3,4},{4,5},{5,6},{6,7},{8,9},{9,10},{10,11},{11... | collective-permute-start | bytes 3068 | tf_op jit(solution)/shard_map/ppermute | solution.py:12
  14.1 0.7 compare_reduce_fusion
  14.8 0.8 slice_convert_fusion
  15.5 32.5 %fusion.3 = (bf16[2048,512]{1,0:T(8,128)(2,1)S(1)}, bf16[2048,512]{1,0:T(8,128)(2,1)S(1)}) fusion(f32[512]{0:T(512)S(1)} %bitcast.125, f32[2048]{0:T(1024)} %param.7, f32[512]{0:T(512)S(1)} %bitcast.124, f32[2048]{0:T(1024)} %param.6, pred[512]{0:T(512)(128)(4,1)S(1)} %compare_reduce_fusion), kind=kLoop, calls=%fused_computation.7 | loop fusion | flops 7340032 | bytes 4215296 | tf_op jit(solution)/shard_map/convert_element_type | solution.py:22
  48.1 1.3 copy-done.4
  49.4 1.0 slice_multiply_fusion
  50.3 4.7 %collective-permute-start.1 = (bf16[255,512]{1,0:T(8,128)(2,1)}, bf16[255,512]{1,0:T(8,128)(2,1)}, u32[]{:S(2)}, u32[]{:S(2)}) collective-permute-start(bf16[255,512]{1,0:T(8,128)(2,1)} %get-tuple-element.54), channel_id=1, source_target_pairs={{0,1},{1,2},{2,3},{3,4},{4,5},{5,6},{6,7},{8,9},{9,10},{10,11},{11... | collective-permute-start | bytes 783368 | tf_op jit(solution)/shard_map/ppermute | solution.py:12
  55.1 2.0 %collective-permute-start = (bf16[255,512]{1,0:T(8,128)(2,1)}, bf16[255,512]{1,0:T(8,128)(2,1)}, u32[]{:S(2)}, u32[]{:S(2)}) collective-permute-start(bf16[255,512]{1,0:T(8,128)(2,1)} %get-tuple-element.55), channel_id=1, source_target_pairs={{0,1},{1,2},{2,3},{3,4},{4,5},{5,6},{6,7},{8,9},{9,10},{10,11},{11... | collective-permute-start | bytes 783368 | tf_op jit(solution)/shard_map/ppermute | solution.py:12
  58.1 0.8 copy.10
  59.2 0.6 eq.375
  59.8 0.6 eq.374
  60.7 0.6 eq.373
  61.2 0.6 eq.372
  62.0 0.6 eq.371
  62.6 0.6 eq.370
  63.5 0.6 eq.369
  64.1 1.2 eq.368
  65.3 0.8 broadcast_select_fusion.9
  66.6 0.8 fusion.109
  67.8 0.8 fusion.119
  69.1 0.8 fusion.117
  70.3 0.8 fusion.115
  71.5 0.8 fusion.113
  72.7 0.8 fusion.111
  73.5 2.0 %broadcast_select_fusion.8 = (bf16[130816]{0:T(1024)(128)(2,1)}, bf16[130816]{0:T(1024)(128)(2,1)S(1)}, bf16[130816]{0:T(1024)(128)(2,1)S(1)}, bf16[130816]{0:T(...) fusion(pred[130816]{0:T(1024)(128)(4,1)S(1)} %eq.375, ...), kind=kLoop, calls=%fused_computation.129 | loop fusion | flops 1308160 | bytes 4447744 | tf_op jit(solution)/shard_map/jit(_where)/select_n | solution.py:64
  75.6 1.4 select_n.266
  77.2 1.4 select_n.280
  78.8 0.5 select_n.278
  79.4 0.5 select_n.276
  80.0 0.5 select_n.274
  80.7 0.7 reshape.322
  82.5 1.6 fusion.21
  84.1 1.4 fusion.20
  88.1 1.3 fusion.157
  89.4 1.0 copy-done.3
  90.4 1.3 fusion.13
  94.6 2.3 %fusion.5 = f32[512,512]{1,0:T(8,128)} fusion(f32[512,512]{1,0:T(8,128)S(1)} %fusion.157, bf16[2048,512]{1,0:T(8,128)(2,1)S(1)} %fusion.6), kind=kOutput, calls=%fused_computation.12 | convolution fusion | flops 1074266112 | bytes 4194304 | tf_op jit(solution)/shard_map/dot_general | solution.py:88
  99.3 0.8 fusion.90
  102.0 0.8 fusion.87
  104.5 2.2 %multiply_reduce_fusion.1 = f32[512]{0:T(512)S(1)} fusion(bf16[2048,512]{1,0:T(8,128)(2,1)} %copy-done), kind=kLoop, calls=%fused_computation.10 | loop fusion | flops 3145216 | bytes 2099200 | tf_op jit(solution)/shard_map/reduce_sum | solution.py:107
  106.7 0.5 multiply_reduce_fusion
  108.0 21.0 %reduce-scatter.3.cloned.1.call-done = f32[64,512]{1,0:T(8,128)} async-done(((f32[512,512]{1,0:T(8,128)}), f32[64,512]{1,0:T(8,128)}) %reduce-scatter.3.cloned.1.call-update) | async-done | bytes 131088 | tf_op jit(solution)/shard_map/reduce_scatter | solution.py:94
  129.0 38.2 %all-reduce.3 = (f32[512]{0:T(512)}, f32[512]{0:T(512)}) all-reduce(f32[512]{0:T(512)S(1)} %add_multiply_fusion.1, f32[512]{0:T(512)S(1)} %add_multiply_fusion), channel_id=1, replica_groups=mesh['grp'=4,'row'=8] {'grp','row'}, use_global_device_ids=true, to_apply=%region_4.5 | all-reduce | flops 1024 | bytes 8192 | tf_op jit(solution)/shard_map/psum | solution.py:109
  167.2 1.4 compare_select_fusion.32
  (192 shorter events, 18.4 us)
Async XLA Ops:
  7.2 121.8 %reduce-scatter.3.cloned.1.call-start = ((), (), s32[]{:S(2)}) async-start(), calls=%async_computation.2 | async-start | bytes 1179648 | tf_op jit(solution)/shard_map/reduce_scatter | solution.py:94
  11.1 88.2 %collective-permute-start.2 = (bf16[2,255]{1,0:T(2,128)(2,1)}, bf16[2,255]{1,0:T(2,128)(2,1)}, u32[]{:S(2)}, u32[]{:S(2)}) collective-permute-start(bf16[2,255]{1,0:T(2,128)(2,1)} %slice_multiply_fusion.2), channel_id=1, source_target_pairs={{0,1},{1,2},{2,3},{3,4},{4,5},{5,6},{6,7},{8,9},{9,10},{10,11},{11... | collective-permute-start | bytes 3068 | tf_op jit(solution)/shard_map/ppermute | solution.py:12
  15.5 41.7 %copy-start.38 = (bf16[2,256]{1,0:T(2,128)(2,1)S(1)}, bf16[2,256]{1,0:T(2,128)(2,1)}, u32[]{:S(2)}) copy-start(bf16[2,256]{1,0:T(2,128)(2,1)} %param.9) | copy-start | bytes 3076
  48.0 1.3 copy-start.4
  48.1 13.8 %copy-start.2 = (bf16[2048,512]{1,0:T(8,128)(2,1)}, bf16[2048,512]{1,0:T(8,128)(2,1)S(1)}, u32[]{:S(2)}) copy-start(bf16[2048,512]{1,0:T(8,128)(2,1)S(1)} %get-tuple-element.32) | copy-start | bytes 6291460
  50.3 39.1 %collective-permute-start.1 = (bf16[255,512]{1,0:T(8,128)(2,1)}, bf16[255,512]{1,0:T(8,128)(2,1)}, u32[]{:S(2)}, u32[]{:S(2)}) collective-permute-start(bf16[255,512]{1,0:T(8,128)(2,1)} %get-tuple-element.54), channel_id=1, source_target_pairs={{0,1},{1,2},{2,3},{3,4},{4,5},{5,6},{6,7},{8,9},{9,10},{10,11},{11... | collective-permute-start | bytes 783368 | tf_op jit(solution)/shard_map/ppermute | solution.py:12
  55.1 27.4 %collective-permute-start = (bf16[255,512]{1,0:T(8,128)(2,1)}, bf16[255,512]{1,0:T(8,128)(2,1)}, u32[]{:S(2)}, u32[]{:S(2)}) collective-permute-start(bf16[255,512]{1,0:T(8,128)(2,1)} %get-tuple-element.55), channel_id=1, source_target_pairs={{0,1},{1,2},{2,3},{3,4},{4,5},{5,6},{6,7},{8,9},{9,10},{10,11},{11... | collective-permute-start | bytes 783368 | tf_op jit(solution)/shard_map/ppermute | solution.py:12
  57.2 3.4 %copy-start.10 = (s32[511]{0:T(512)}, s32[511]{0:T(512)S(1)}, u32[]{:S(2)}) copy-start(s32[511]{0:T(512)S(1)} %get-tuple-element.42) | copy-start | bytes 6136
  57.2 3.4 %copy-start.12 = (s32[511]{0:T(512)}, s32[511]{0:T(512)S(1)}, u32[]{:S(2)}) copy-start(s32[511]{0:T(512)S(1)} %get-tuple-element.43) | copy-start | bytes 6136
  57.2 6.0 %copy-start.14 = (s32[511]{0:T(512)}, s32[511]{0:T(512)S(1)}, u32[]{:S(2)}) copy-start(s32[511]{0:T(512)S(1)} %get-tuple-element.44) | copy-start | bytes 6136
  57.2 6.0 %copy-start.16 = (s32[511]{0:T(512)}, s32[511]{0:T(512)S(1)}, u32[]{:S(2)}) copy-start(s32[511]{0:T(512)S(1)} %get-tuple-element.45) | copy-start | bytes 6136
  57.2 6.2 %copy-start.18 = (s32[511]{0:T(512)}, s32[511]{0:T(512)S(1)}, u32[]{:S(2)}) copy-start(s32[511]{0:T(512)S(1)} %get-tuple-element.46) | copy-start | bytes 6136
  57.3 6.2 %copy-start.20 = (s32[511]{0:T(512)}, s32[511]{0:T(512)S(1)}, u32[]{:S(2)}) copy-start(s32[511]{0:T(512)S(1)} %get-tuple-element.47) | copy-start | bytes 6136
  57.3 6.2 %copy-start.22 = (s32[511]{0:T(512)}, s32[511]{0:T(512)S(1)}, u32[]{:S(2)}) copy-start(s32[511]{0:T(512)S(1)} %get-tuple-element.48) | copy-start | bytes 6136
  57.9 2.7 %copy-start.24 = (s32[256]{0:T(256)}, s32[256]{0:T(256)S(1)}, u32[]{:S(2)}) copy-start(s32[256]{0:T(256)S(1)} %get-tuple-element.34) | copy-start | bytes 3076
  57.9 2.7 %copy-start.26 = (s32[256]{0:T(256)}, s32[256]{0:T(256)S(1)}, u32[]{:S(2)}) copy-start(s32[256]{0:T(256)S(1)} %get-tuple-element.35) | copy-start | bytes 3076
  57.9 2.7 %copy-start.28 = (s32[256]{0:T(256)}, s32[256]{0:T(256)S(1)}, u32[]{:S(2)}) copy-start(s32[256]{0:T(256)S(1)} %get-tuple-element.36) | copy-start | bytes 3076
  57.9 2.7 %copy-start.30 = (s32[256]{0:T(256)}, s32[256]{0:T(256)S(1)}, u32[]{:S(2)}) copy-start(s32[256]{0:T(256)S(1)} %get-tuple-element.37) | copy-start | bytes 3076
  57.9 5.6 %copy-start.32 = (s32[256]{0:T(256)}, s32[256]{0:T(256)S(1)}, u32[]{:S(2)}) copy-start(s32[256]{0:T(256)S(1)} %get-tuple-element.38) | copy-start | bytes 3076
  57.9 5.6 %copy-start.34 = (s32[256]{0:T(256)}, s32[256]{0:T(256)S(1)}, u32[]{:S(2)}) copy-start(s32[256]{0:T(256)S(1)} %get-tuple-element.39) | copy-start | bytes 3076
  57.9 5.6 %copy-start.36 = (s32[256]{0:T(256)}, s32[256]{0:T(256)S(1)}, u32[]{:S(2)}) copy-start(s32[256]{0:T(256)S(1)} %get-tuple-element.40) | copy-start | bytes 3076
  63.2 3.4 %copy-start.9 = (bf16[2,2048]{1,0:T(2,128)(2,1)S(1)}, bf16[2,2048]{1,0:T(2,128)(2,1)}, u32[]{:S(2)}) copy-start(bf16[2,2048]{1,0:T(2,128)(2,1)} %param.8) | copy-start | bytes 24580
  66.6 6.9 %copy-start.7 = (bf16[32,4,8,128]{3,1,2,0:T(4,128)(2,1)S(1)}, bf16[32,4,8,128]{3,1,2,0:T(4,128)(2,1)}, u32[]{:S(2)}) copy-start(bf16[32,4,8,128]{3,1,2,0:T(4,128)(2,1)} %copy.10) | copy-start | bytes 786436
  75.6 5.1 %copy-start.8 = (bf16[130816]{0:T(1024)(128)(2,1)S(1)}, bf16[130816]{0:T(1024)(128)(2,1)}, u32[]{:S(2)}) copy-start(bf16[130816]{0:T(1024)(128)(2,1)} %get-tuple-element.31) | copy-start | bytes 784900
  81.4 2.7 %copy-start.23 = (s32[511]{0:T(512)S(1)}, s32[511]{0:T(512)}, u32[]{:S(2)}) copy-start(s32[511]{0:T(512)} %copy-done.22) | copy-start | bytes 6136
  81.4 2.7 %copy-start.37 = (s32[256]{0:T(256)S(1)}, s32[256]{0:T(256)}, u32[]{:S(2)}) copy-start(s32[256]{0:T(256)} %copy-done.36) | copy-start | bytes 3076
  82.5 3.1 %copy-start.5 = (bf16[2048,512]{1,0:T(8,128)(2,1)S(1)}, bf16[2048,512]{1,0:T(8,128)(2,1)}, u32[]{:S(2)}) copy-start(bf16[2048,512]{1,0:T(8,128)(2,1)} %copy-done.4) | copy-start | bytes 6291460
  82.5 3.1 %copy-start.21 = (s32[511]{0:T(512)S(1)}, s32[511]{0:T(512)}, u32[]{:S(2)}) copy-start(s32[511]{0:T(512)} %copy-done.20) | copy-start | bytes 6136
  82.5 3.1 %copy-start.35 = (s32[256]{0:T(256)S(1)}, s32[256]{0:T(256)}, u32[]{:S(2)}) copy-start(s32[256]{0:T(256)} %copy-done.34) | copy-start | bytes 3076
  84.1 1.9 %copy-start.19 = (s32[511]{0:T(512)S(1)}, s32[511]{0:T(512)}, u32[]{:S(2)}) copy-start(s32[511]{0:T(512)} %copy-done.18) | copy-start | bytes 6136
  84.1 1.9 %copy-start.33 = (s32[256]{0:T(256)S(1)}, s32[256]{0:T(256)}, u32[]{:S(2)}) copy-start(s32[256]{0:T(256)} %copy-done.32) | copy-start | bytes 3076
  85.5 0.8 copy-start.17
  85.6 0.8 copy-start.31
  86.0 0.8 copy-start.15
  86.0 0.8 copy-start.29
  86.4 0.8 copy-start.13
  86.4 0.8 copy-start.27
  88.1 1.3 copy-start
  88.1 2.3 %copy-start.3 = (bf16[2048,512]{1,0:T(8,128)(2,1)S(1)}, bf16[2048,512]{1,0:T(8,128)(2,1)}, u32[]{:S(2)}) copy-start(bf16[2048,512]{1,0:T(8,128)(2,1)} %copy-done.2) | copy-start | bytes 6291460
  94.5 2.4 %copy-start.39 = (f32[1,256]{1,0:T(1,128)S(1)}, f32[1,256]{1,0:T(1,128)}, u32[]{:S(2)}) copy-start(f32[1,256]{1,0:T(1,128)} %fusion.109) | copy-start | bytes 3076
  94.5 2.5 %copy-start.40 = (f32[1,256]{1,0:T(1,128)S(1)}, f32[1,256]{1,0:T(1,128)}, u32[]{:S(2)}) copy-start(f32[1,256]{1,0:T(1,128)} %fusion.119) | copy-start | bytes 3076
  94.5 2.5 %copy-start.41 = (f32[1,256]{1,0:T(1,128)S(1)}, f32[1,256]{1,0:T(1,128)}, u32[]{:S(2)}) copy-start(f32[1,256]{1,0:T(1,128)} %fusion.117) | copy-start | bytes 3076
  94.5 2.5 %copy-start.42 = (f32[1,256]{1,0:T(1,128)S(1)}, f32[1,256]{1,0:T(1,128)}, u32[]{:S(2)}) copy-start(f32[1,256]{1,0:T(1,128)} %fusion.115) | copy-start | bytes 3076
  94.5 2.5 %copy-start.43 = (f32[1,256]{1,0:T(1,128)S(1)}, f32[1,256]{1,0:T(1,128)}, u32[]{:S(2)}) copy-start(f32[1,256]{1,0:T(1,128)} %fusion.113) | copy-start | bytes 3076
  94.5 2.5 %copy-start.44 = (f32[1,256]{1,0:T(1,128)S(1)}, f32[1,256]{1,0:T(1,128)}, u32[]{:S(2)}) copy-start(f32[1,256]{1,0:T(1,128)} %fusion.111) | copy-start | bytes 3076
  94.5 2.5 %copy-start.6 = (bf16[130816]{0:T(1024)(128)(2,1)S(1)}, bf16[130816]{0:T(1024)(128)(2,1)}, u32[]{:S(2)}) copy-start(bf16[130816]{0:T(1024)(128)(2,1)} %get-tuple-element.22) | copy-start | bytes 784900
  96.8 70.3 %reduce-scatter.5.cloned.1.call-start = ((), (), s32[]{:S(2)}) async-start(), calls=%async_computation.3 | async-start | bytes 163840 | tf_op jit(solution)/shard_map/reduce_scatter | solution.py:95
  104.5 2.8 %copy-start.1 = (bf16[2048,512]{1,0:T(8,128)(2,1)S(1)}, bf16[2048,512]{1,0:T(8,128)(2,1)}, u32[]{:S(2)}) copy-start(bf16[2048,512]{1,0:T(8,128)(2,1)} %copy-done) | copy-start | bytes 6291460
  (2 other events, 1.6 us)
Sparse Core Ops, SparseCore 0:
  97.0 31.9 reduce-scatter.2
  131.7 22.3 reduce-scatter.4
where the time goes:
time: 177 us; the launch traced here: 175 us
  other arithmetic  46.2 us (26%)
  blocking collectives  38.2 us (22%)
  local copies, waits for them, and re-layouts  23.9 us (14%)
  matrix products  21.3 us (12%)
  waiting for transfers between devices  21 us (12%)
  between operations  15.1 us (9%)
  starting transfers between devices  9.72 us (5%)
    psum x1, blocking collectives, on_device(): lax.psum((rhs_term * gram_scale, square_term * row_scale), ('grp', 'row'))  38.2 us
    convert_element_type x1, other arithmetic, design_rows(): along = (jnp.sin(polar_angle) * azimuth_wave).astype(jnp.bfloat16)  32.5 us
    reduce_scatter x1, waiting for transfers between devices, on_device(): lax.psum_scatter(gram_sum * gram_scale, 'row', scatter_dimension=0, tiled...  21 us
    ppermute x3, starting transfers between devices, passed_along(): return lax.ppermute(array, axis, pairs)  9.64 us
    dot_general x16, matrix products, on_device(): jnp.dot(matrix, windows[component][block_low:block_low + 2 * tap_count -...  9.28 us
    select_n x16, local copies, waits for them, and re-layouts, on_device(): matrix = jnp.where(valid_mask, tap_table, jnp.zeros((), tap_table.dtype))  9.1 us
    dot_general x16, matrix products, on_device(): jnp.dot(matrix, signal_window[component, block_low:block_low + 2 * tap_co...  7.77 us
    unnamed x108, local copies, waits for them, and re-layouts  6.59 us
  transfers between devices with their start and end apart: 5, of which 1 were waited for; matrix products, arithmetic and copies ran while one was open for 48% of the time, Pallas kernels for 0%

commit v1 on v0

v1 whole, which is shorter than its diff:
```python
import functools
import math

import jax
import jax.numpy as jnp
from jax import lax
from jax.experimental import pallas as pl
from jax.experimental.pallas import tpu as pltpu
from jax.sharding import PartitionSpec as P

F32 = jnp.float32
BF16 = jnp.bfloat16
LANES = 128
EXTRA = 16
CHUNK = 64
SIN_C = (4.442866325378418, -7.307384967803955, 3.594230890274048, -0.7829042077064514)
COS_C = (1.41420316696167, -6.977553367614746, 5.714066982269287, -1.7246402502059937)
TURN_HIGH = 2608.0 / 16384.0
TURN_LOW = 1.0 / (2.0 * math.pi) - TURN_HIGH
FUSED = True


def poly(u, coefficients):
    total = coefficients[-1]
    for c in coefficients[-2::-1]:
        total = total * u + c
    return total


def turns(angle):
    head = jnp.round(angle * 1024.0) * (1.0 / 1024.0)
    tail = angle - head
    coarse = head * TURN_HIGH
    high = jnp.round(coarse * 32768.0) * (1.0 / 32768.0)
    low = (coarse - high) + (head * TURN_LOW + tail * (TURN_HIGH + TURN_LOW))
    return high, low


def local_kernel(
    fused, n_grp, n_row, blocks, taps_n, width,
    col_ref, lon_ref, obs_ref, taps_ref, seg_ref, har_ref, *refs,
):
    if fused:
        (out_ref, small_ref, design, filt, table, matrix, lab_col, lab, waves, gram,
         halo_send, halo, sa, ra, sb, rb, sc, rc, sd, rd, rs, rr, rz, send_sem, recv_sem) = refs
    else:
        (halo, gram, small_ref, design, filt, table, matrix, lab_col, lab, waves) = refs
    per = taps_n // LANES
    col_tiles = width // LANES
    row_index = lax.axis_index("row")
    grp_index = lax.axis_index("grp")

    if fused:
        core = lax.rem(row_index, 2)
        z = row_index // 2
        y = grp_index // 2
        x = lax.rem(grp_index, 2)
        n_z = n_row // 2
        twin = (grp_index, row_index + 1 - 2 * core)
        y_peer = (lax.rem(grp_index + 2, 4), row_index)
        x_peer = (grp_index + 1 - 2 * x, row_index)
        z_peers = [(grp_index, lax.rem(row_index + 2 * k, n_row)) for k in range(1, n_z)]
        after = (grp_index, lax.rem(row_index + 1, n_row))
        before = (grp_index, lax.rem(row_index + n_row - 1, n_row))
        greeted = [twin, y_peer, x_peer, after, before] + z_peers
        barrier = pltpu.get_barrier_semaphore()
        for peer in greeted:
            pl.semaphore_signal(barrier, inc=1, device_id=peer, device_id_type=pl.DeviceIdType.MESH)
        pl.semaphore_wait(barrier, len(greeted))

        def copy(src, dst, number, peer):
            c = pltpu.make_async_remote_copy(
                src_ref=src, dst_ref=dst,
                send_sem=send_sem.at[number], recv_sem=recv_sem.at[number],
                device_id=peer, device_id_type=pl.DeviceIdType.MESH,
            )
            c.start()
            return c

        last = blocks * per - per
        halo_send[0:per] = col_ref[last:last + per]
        halo_send[per:2 * per] = lon_ref[last:last + per]
        halo_send[2 * per:3 * per] = seg_ref[last:last + per].astype(F32)
        for c in range(2):
            for p in range(per):
                at = (last + p) * LANES
                halo_send[(3 + c) * per + p:(3 + c) * per + p + 1] = obs_ref[
                    c:c + 1, at:at + LANES].astype(F32)
        halo_send[5 * per:] = jnp.zeros((halo_send.shape[0] - 5 * per, LANES), F32)
        halo_copy = copy(halo_send, halo, 0, after)

    degree = har_ref[0:1, :].astype(F32)
    order = har_ref[1:2, :]
    size = jnp.abs(order).astype(F32)
    phase = jnp.where(order >= 0, 0.0, -0.25).astype(F32)
    for number, values in enumerate((degree, size, phase)):
        for t in range(col_tiles):
            here = slice(t * LANES, (t + 1) * LANES)
            waves[number, here, :] = jnp.broadcast_to(values[:, here], (LANES, LANES)).T

    j = lax.broadcasted_iota(jnp.int32, (taps_n, taps_n), 0)
    i = lax.broadcasted_iota(jnp.int32, (taps_n, taps_n), 1)
    for c in range(2):
        row = jnp.broadcast_to(taps_ref[c:c + 1, :].astype(F32), (taps_n, taps_n))
        around = pltpu.roll(row, 0, 1, stride=1, stride_axis=0)
        table[c, 0:taps_n, :] = jnp.where(i < j, around, 0.0)
        table[c, taps_n:, :] = jnp.where(i >= j, around, 0.0)

    upper = (
        lax.broadcasted_iota(jnp.int32, (LANES, LANES), 0)
        <= lax.broadcasted_iota(jnp.int32, (LANES, LANES), 1)
    ).astype(BF16)
    within = jnp.dot(seg_ref[...].astype(F32).astype(BF16), upper, preferred_element_type=F32)
    offset = jnp.zeros((1, 1), F32)
    for r in range(blocks * per):
        lab[per + r:per + r + 1, :] = within[r:r + 1] + offset
        offset = offset + within[r:r + 1, LANES - 1:]

    def label_columns(tile):
        at = pl.multiple_of(tile * LANES, LANES)
        lab_col[pl.ds(at, LANES), :] = jnp.broadcast_to(lab[pl.ds(tile, 1), :], (LANES, LANES)).T

    @pl.loop(per, (blocks + 1) * per)
    def _(tile):
        label_columns(tile)

    def design_tile(theta, phi, tile):
        at = pl.multiple_of(tile * LANES, LANES)
        theta_high, theta_low = turns(theta)
        phi_high, phi_low = turns(phi)

        @pl.loop(0, width // CHUNK)
        def _(chunk):
            rows = pl.ds(pl.multiple_of(chunk * CHUNK, CHUNK), CHUNK)
            n = waves[0, rows, :]
            m = waves[1, rows, :]
            a = n * theta_high
            a = (a - jnp.round(a)) + n * theta_low
            b = m * phi_high + waves[2, rows, :]
            b = (b - jnp.round(b)) + m * phi_low
            ua = a * a
            ub = b * b
            sin_a = a * poly(ua, SIN_C)
            cos_a = poly(ua, COS_C)
            sin_b = b * poly(ub, SIN_C)
            w = 1.0 - sin_b * sin_b
            design[0, rows, pl.ds(at, LANES)] = ((1.0 - sin_a * sin_a) * w).astype(BF16)
            design[1, rows, pl.ds(at, LANES)] = ((sin_a * cos_a) * w).astype(BF16)

    below = lax.broadcasted_iota(jnp.int32, (EXTRA, LANES), 0) == 0

    def signal_tile(values, c, tile):
        at = pl.multiple_of(tile * LANES, LANES)
        design[c, width:, pl.ds(at, LANES)] = jnp.where(
            below, jnp.broadcast_to(values, (EXTRA, LANES)), 0.0
        ).astype(BF16)

    @pl.loop(0, blocks * per)
    def _(tile):
        design_tile(col_ref[pl.ds(tile, 1), :], lon_ref[pl.ds(tile, 1), :], tile + per)
        for c in range(2):
            at = pl.multiple_of(tile * LANES, LANES)
            signal_tile(obs_ref[c:c + 1, pl.ds(at, LANES)].astype(F32), c, tile + per)

    if fused:
        halo_copy.wait()
    counts = jnp.dot(
        halo[2 * per:3 * per].astype(BF16), upper, preferred_element_type=F32
    )
    offset = jnp.zeros((1, 1), F32)
    rows = []
    for r in range(per):
        rows.append(counts[r:r + 1] + offset)
        offset = offset + counts[r:r + 1, LANES - 1:]
    first = row_index == 0
    for r in range(per):
        lab[r:r + 1, :] = jnp.where(first, -1.0, rows[r] - offset)
        label_columns(r)

    @pl.loop(0, per)
    def _(tile):
        design_tile(halo[pl.ds(tile, 1), :], halo[pl.ds(per + tile, 1), :], tile)
        for c in range(2):
            signal_tile(halo[pl.ds((3 + c) * per + tile, 1), :], c, tile)

    epochs = blocks * taps_n

    @pl.loop(0, blocks)
    def _(block):
        window = pl.multiple_of(block * taps_n, taps_n)
        for half in range(per):
            lanes = slice(half * LANES, (half + 1) * LANES)
            out_label = lab[pl.ds((block + 1) * per + half, 1), :]
            for part in range(2 * taps_n // LANES):
                at = slice(part * LANES, (part + 1) * LANES)
                same = lab_col[pl.ds(window + part * LANES, LANES), :] == out_label
                for c in range(2):
                    matrix[c, at, lanes] = jnp.where(same, table[c, at, lanes], 0.0).astype(BF16)
        for c in range(2):
            filt[:, pl.ds(pl.multiple_of(c * epochs + window, taps_n), taps_n)] = jnp.dot(
                design[c, :, pl.ds(window, 2 * taps_n)], matrix[c],
                preferred_element_type=F32,
            ).astype(BF16)

    half_width = width // 2
    half_tiles = half_width // LANES
    depth = min(1024, 2 * epochs)
    copies_a = []
    for half in range(2):
        gram[half * half_tiles:(half + 1) * half_tiles] = jnp.zeros(
            (half_tiles, width + EXTRA, LANES), F32
        )

        @pl.loop(0, 2 * epochs // depth)
        def _(step):
            at = pl.ds(pl.multiple_of(step * depth, depth), depth)
            part = lax.dot_general(
                filt[:, at], filt[half * half_width:(half + 1) * half_width, at],
                (((1,), (1,)), ((), ())), preferred_element_type=F32,
            )
            for t in range(half_tiles):
                gram[half * half_tiles + t] += part[:, t * LANES:(t + 1) * LANES]

        if fused:
            tile_rows = width // n_row
            for t in range(half * half_tiles, (half + 1) * half_tiles):
                for zz in range(n_z):
                    at = pl.multiple_of((2 * zz + 1 - core) * tile_rows, tile_rows)
                    sa[t, zz] = gram[t, pl.ds(at, tile_rows), :].astype(BF16)
            part = pl.ds(half * half_tiles, half_tiles)
            copies_a.append(copy(sa.at[part], ra.at[part], 1 + half, twin))

    eye = lax.broadcasted_iota(jnp.int32, (LANES, LANES), 0) == lax.broadcasted_iota(
        jnp.int32, (LANES, LANES), 1
    )
    small = []
    for t in range(col_tiles):
        small.append(gram[t, width:width + 1, :])
    for t in range(col_tiles):
        square = gram[t, t * LANES:(t + 1) * LANES, :]
        small.append(jnp.sum(jnp.where(eye, square, 0.0), axis=0, keepdims=True))
    if not fused:
        for r, row in enumerate(small):
            small_ref[r:r + 1, :] = row
        return

    for r, row in enumerate(small):
        rs[0, r:r + 1, :] = row
    small_a = copy(rs.at[0], rr.at[0], 3, twin)
    for c in copies_a:
        c.wait()
    for t in range(col_tiles):
        for zz in range(n_z):
            at = pl.multiple_of((2 * zz + core) * tile_rows, tile_rows)
            gram[t, pl.ds(zz * tile_rows, tile_rows), :] = gram[
                t, pl.ds(at, tile_rows), :] + ra[t, zz].astype(F32)

    def held(t, zz):
        return gram[t, pl.ds(pl.multiple_of(zz * tile_rows, tile_rows), tile_rows), :]

    def add(t, zz, values):
        at = pl.ds(pl.multiple_of(zz * tile_rows, tile_rows), tile_rows)
        gram[t, at, :] = gram[t, at, :] + values.astype(F32)

    z_half = n_z // 2
    for k in range(2):
        for q in range(z_half):
            sb[0, k, q] = held(2 * (1 - y) + k, q).astype(BF16)
            sb[1, k, q] = held(2 * k + 1 - x, z_half + q).astype(BF16)
    copies_b = [copy(sb.at[0], rb.at[0], 4, y_peer), copy(sb.at[1], rb.at[1], 5, x_peer)]
    small_a.wait()
    rs[1] = rs[0] + rr[0]
    small_b = copy(rs.at[1], rr.at[1], 6, y_peer)
    copies_b[0].wait()
    for q in range(z_half):
        sc[0, q] = (held(2 * y + 1 - x, q) + rb[0, 1 - x, q].astype(F32)).astype(BF16)
    copies_c = [copy(sc.at[0], rc.at[0], 7, x_peer)]
    copies_b[1].wait()
    for q in range(z_half):
        sc[1, q] = (held(2 * (1 - y) + x, z_half + q) + rb[1, 1 - y, q].astype(F32)).astype(BF16)
    copies_c.append(copy(sc.at[1], rc.at[1], 8, y_peer))
    for q in range(z_half):
        add(grp_index, q, rb[0, x, q])
        add(grp_index, z_half + q, rb[1, y, q])
    small_b.wait()
    rs[2] = rs[1] + rr[1]
    small_c = copy(rs.at[2], rr.at[2], 9, x_peer)
    for s in range(2):
        copies_c[s].wait()
        for q in range(z_half):
            add(grp_index, s * z_half + q, rc[s, q])
    copies_d = []
    for k in range(1, n_z):
        sd[k - 1] = held(grp_index, lax.rem(z + k, n_z)).astype(BF16)
        copies_d.append(copy(sd.at[k - 1], rd.at[k - 1], 9 + k, z_peers[k - 1]))
    small_c.wait()
    rz[z] = rs[2] + rr[2]
    small_d = []
    for k in range(1, n_z):
        small_d.append(copy(rz.at[z], rz.at[z], 8 + n_z + k, z_peers[k - 1]))
    total = held(grp_index, z)
    for k in range(1, n_z):
        copies_d[k - 1].wait()
        total = total + rd[k - 1].astype(F32)
    out_ref[...] = total
    for c in small_d:
        c.wait()
    total = rz[0]
    for zz in range(1, n_z):
        total = total + rz[zz]
    small_ref[...] = total


def on_device(colatitude, longitude, observed, filter_taps, segment_start, harmonic):
    rows_here = colatitude.shape[0]
    taps_n = filter_taps.shape[1]
    width = harmonic.shape[1]
    n_grp = lax.axis_size("grp")
    n_row = lax.axis_size("row")
    blocks = rows_here // taps_n
    per = taps_n // LANES
    tiles = width // LANES
    rows_total = rows_here * n_grp * n_row
    row_scale = 1.0 / rows_total
    gram_scale = 1.0 / math.sqrt(rows_total)
    fused = FUSED and n_grp == 4 and n_row == 8 and width == n_grp * LANES
    split = [a.reshape(rows_here // LANES, LANES) for a in (colatitude, longitude, segment_start)]
    inputs = [split[0], split[1], observed, filter_taps, split[2], harmonic]
    window = rows_here + taps_n
    scratch = [
        pltpu.VMEM((2, width + EXTRA, window), BF16),
        pltpu.VMEM((width + EXTRA, 2 * rows_here), BF16),
        pltpu.VMEM((2, 2 * taps_n, taps_n), F32),
        pltpu.VMEM((2, 2 * taps_n, taps_n), BF16),
        pltpu.VMEM((window, LANES), F32),
        pltpu.VMEM((window // LANES, LANES), F32),
        pltpu.VMEM((3, width, LANES), F32),
    ]
    gram_shape = (tiles, width + EXTRA, LANES)
    small_shape = jax.ShapeDtypeStruct((2 * tiles, LANES), F32)
    halo_shape = (8 * per, LANES)
    if fused:
        tile_rows = width // n_row
        n_z = n_row // 2
        tile = (tile_rows, LANES)
        copies = 9 + 2 * n_z
        scratch += [
            pltpu.VMEM(gram_shape, F32),
            pltpu.VMEM(halo_shape, F32),
            pltpu.VMEM(halo_shape, F32),
            pltpu.VMEM((tiles, n_z) + tile, BF16),
            pltpu.VMEM((tiles, n_z) + tile, BF16),
            pltpu.VMEM((2, 2, n_z // 2) + tile, BF16),
            pltpu.VMEM((2, 2, n_z // 2) + tile, BF16),
            pltpu.VMEM((2, n_z // 2) + tile, BF16),
            pltpu.VMEM((2, n_z // 2) + tile, BF16),
            pltpu.VMEM((n_z - 1,) + tile, BF16),
            pltpu.VMEM((n_z - 1,) + tile, BF16),
            pltpu.VMEM((3, 2 * tiles, LANES), F32),
            pltpu.VMEM((3, 2 * tiles, LANES), F32),
            pltpu.VMEM((n_z, 2 * tiles, LANES), F32),
            pltpu.SemaphoreType.DMA((copies,)),
            pltpu.SemaphoreType.DMA((copies,)),
        ]
        main_shape = jax.ShapeDtypeStruct((tile_rows, LANES), F32)
    else:
        last = rows_here // LANES - per
        pieces = [split[0][last:], split[1][last:], split[2][last:].astype(F32)]
        pieces.append(observed[:, rows_here - taps_n:].astype(F32).reshape(2 * per, LANES))
        pieces.append(jnp.zeros((3 * per, LANES), F32))
        pairs = [(k, k + 1) for k in range(n_row - 1)]
        inputs.append(lax.ppermute(jnp.concatenate(pieces), "row", pairs))
        main_shape = jax.ShapeDtypeStruct(gram_shape, F32)
    params = dict(vmem_limit_bytes=40 * 1024 * 1024)
    if fused:
        params.update(collective_id=0, has_side_effects=True)
    main, small = pl.pallas_call(
        functools.partial(local_kernel, fused, n_grp, n_row, blocks, taps_n, width),
        out_shape=(main_shape, small_shape),
        in_specs=[pl.BlockSpec(memory_space=pltpu.VMEM)] * len(inputs),
        out_specs=(pl.BlockSpec(memory_space=pltpu.VMEM),) * 2,
        scratch_shapes=scratch,
        compiler_params=pltpu.CompilerParams(**params),
        name="normal_equations",
    )(*inputs)
    if fused:
        normal = main
    else:
        gram = main[:, :width].transpose(1, 0, 2).reshape(width, width)
        owned = lax.psum_scatter(gram, "row", scatter_dimension=0, tiled=True)
        normal = lax.psum_scatter(owned, "grp", scatter_dimension=1, tiled=True)
        small = lax.psum(small, ("grp", "row"))
    row_at = lax.axis_index("row") * normal.shape[0] + lax.broadcasted_iota(
        jnp.int32, normal.shape, 0
    )
    col_at = lax.axis_index("grp") * normal.shape[1] + lax.broadcasted_iota(
        jnp.int32, normal.shape, 1
    )
    normal = jnp.where(row_at == col_at, 0.0, normal * gram_scale)
    right_side = small[:tiles].reshape(width) * gram_scale
    diagonal = small[tiles:].reshape(width) * row_scale
    return (normal, right_side, diagonal)


def solution(mesh):
    placed = (
        P(("grp", "row")),
        P(("grp", "row")),
        P(None, ("grp", "row")),
        P(),
        P(("grp", "row")),
        P(),
    )
    return jax.shard_map(
        on_device,
        mesh=mesh,
        in_specs=placed,
        out_specs=(P("row", "grp"), P(), P()),
        check_vma=False,
    )
```

time: 177 us -> 40.5 us (0.23)
  other arithmetic: 46.2 us -> 1.29 us
  blocking collectives: 38.2 us -> 0 us
  Pallas kernels: 0 us -> 35.4 us
  matrix products: 21.3 us -> 0 us
  local copies, waits for them, and re-layouts: 23.9 us -> 2.74 us
  waiting for transfers between devices: 21 us -> 0 us
  between operations: 15.1 us -> 0.69 us
  starting transfers between devices: 9.72 us -> 0 us
    psum x1 -> x0, blocking collectives: 38.2 us -> none  [on_device(): lax.psum((rhs_term * gram_scale, square_term * row_scale), ('grp', 'row'))]
    pallas_call x0 -> x1, Pallas kernels: none -> 35.4 us  [on_device(): pl.pallas_call(functools.partial(local_kernel, fused, n_grp, n_row, block...]
    convert_element_type x19 -> x0, other arithmetic: 34 us -> none  [the longest x1 32.5 us: design_rows(): along = (jnp.sin(polar_angle) * azimuth_wave).astype(jnp.bfloat16)]
    dot_general x36 -> x0, matrix products: 21.3 us -> none  [the longest x16 9.28 us: on_device(): jnp.dot(matrix, windows[component][block_low:block_low + 2 * tap_count -...]
    reduce_scatter x2 -> x0, waiting for transfers between devices: 21 us -> none  [the longest x1 21 us: on_device(): lax.psum_scatter(gram_sum * gram_scale, 'row', scatter_dimension=0, tiled...]
    ppermute x3 -> x0, starting transfers between devices: 9.64 us -> none  [passed_along(): return lax.ppermute(array, axis, pairs)]
    select_n x16 -> x0, local copies, waits for them, and re-layouts: 9.1 us -> none  [on_device(): matrix = jnp.where(valid_mask, tap_table, jnp.zeros((), tap_table.dtype))]
    eq x9 -> x0, local copies, waits for them, and re-layouts: 5.28 us -> none  [on_device(): valid_mask = out_label[:, None] == in_label[None, :]]
  transfers between devices with their start and end apart: 5 -> 0, of which waited for: 1 -> 0; matrix products, arithmetic and copies ran while one was open for 48% -> 0% of each run, Pallas kernels for 0% -> 0%
where the time goes in v1:
time: 40.5 us; the launch traced here: 40.1 us
  Pallas kernels  35.4 us (87%)
  local copies, waits for them, and re-layouts  2.74 us (7%)
  other arithmetic  1.29 us (3%)
  between operations  0.69 us (2%)
    pallas_call x1, Pallas kernels, on_device(): pl.pallas_call(functools.partial(local_kernel, fused, n_grp, n_row, block...  35.4 us
    unnamed x12, local copies, waits for them, and re-layouts  2.74 us

profile of v1, /device:TPU:0, one launch (start us, length us, event | category | flops | bytes accessed | tf_op | source)
XLA Modules:
  0.0 40.1 jit_solution(8954285832462034445)
XLA Ops:
  0.6 0.0 copy-start.2
  0.6 0.0 copy-start.1
  0.7 0.0 copy-start
  0.7 0.6 %copy-done.2 = bf16[2,2048]{1,0:T(2,128)(2,1)S(1)} copy-done((bf16[2,2048]{1,0:T(2,128)(2,1)S(1)}, bf16[2,2048]{1,0:T(2,128)(2,1)}, u32[]{:S(2)}) %copy-start.2) | copy-done | bytes 8216
  1.3 0.0 copy-done.1
  1.3 0.0 copy-done
  1.4 0.0 copy-start.3
  1.4 0.7 %copy-done.3 = s32[2048]{0:T(1024)S(1)} copy-done((s32[2048]{0:T(1024)S(1)}, s32[2048]{0:T(1024)}, u32[]{:S(2)}) %copy-start.3) | copy-done | bytes 8216
  2.1 0.0 copy-start.4
  2.1 0.7 %copy-done.4 = s32[2,512]{1,0:T(2,128)S(1)} copy-done((s32[2,512]{1,0:T(2,128)S(1)}, s32[2,512]{1,0:T(2,128)}, u32[]{:S(2)}) %copy-start.4) | copy-done | bytes 4120
  2.7 0.0 copy-start.5
  2.7 0.7 %copy-done.5 = bf16[2,256]{1,0:T(2,128)(2,1)S(1)} copy-done((bf16[2,256]{1,0:T(2,128)(2,1)S(1)}, bf16[2,256]{1,0:T(2,128)(2,1)}, u32[]{:S(2)}) %copy-start.5) | copy-done | bytes 1048
  3.4 35.4 %normal_equations.1 = (f32[64,128]{1,0:T(8,128)S(1)}, f32[8,128]{1,0:T(8,128)S(1)}) custom-call(f32[16,128]{1,0:T(8,128)S(1)} %bitcast.7, f32[16,128]{1,0:T(8,128)S(1)} %bitcast.8, bf16[2,2048]{1,0:T(2,128)(2,1)S(1)} %copy-done.2, bf16[2,256]{1,0:T(2,128)(2,1)S(1)} %copy-done.5, s32[16,128]{1,0:T(8,128)S(1)} %bitcast.9, s32[2,512]{1,0:T(2,128)S(1)} %copy-done.4), custom_call_target="tpu_custom_call" | custom-call | tf_op jit(solution)/shard_map/normal_equations/pallas_call | solution.py:377
  38.8 0.7 %multiply_select_fusion = f32[64,128]{1,0:T(8,128)} fusion(f32[64,128]{1,0:T(8,128)S(1)} %get-tuple-element.5, s32[128]{0:T(128)S(1)} %iota_add_fusion, s32[64]{0:T(128)S(1)} %iota_add_fusion.1), kind=kLoop, calls=%fused_computation | loop fusion | flops 24576 | bytes 66304 | tf_op jit(solution)/shard_map/jit(_where)/select_n | solution.py:399
  39.5 0.6 %multiply_bitcast_fusion = (f32[512]{0:T(512)}, f32[512]{0:T(512)}) fusion(f32[8,128]{1,0:T(8,128)S(1)} %get-tuple-element.6), kind=kLoop, calls=%fused_computation.1 | loop fusion | flops 1024 | bytes 8192 | tf_op jit(solution)/shard_map/mul | solution.py:401
  (2 shorter events, 0.0 us)
Async XLA Ops:
  0.6 0.7 %copy-start.2 = (bf16[2,2048]{1,0:T(2,128)(2,1)S(1)}, bf16[2,2048]{1,0:T(2,128)(2,1)}, u32[]{:S(2)}) copy-start(bf16[2,2048]{1,0:T(2,128)(2,1)} %obs_ref.1) | copy-start | bytes 24580
  0.6 0.7 %copy-start.1 = (f32[2048]{0:T(1024)S(1)}, f32[2048]{0:T(1024)}, u32[]{:S(2)}) copy-start(f32[2048]{0:T(1024)} %param.7) | copy-start | bytes 24580
  0.7 0.7 %copy-start = (f32[2048]{0:T(1024)S(1)}, f32[2048]{0:T(1024)}, u32[]{:S(2)}) copy-start(f32[2048]{0:T(1024)} %param.6) | copy-start | bytes 24580
  1.4 0.7 %copy-start.3 = (s32[2048]{0:T(1024)S(1)}, s32[2048]{0:T(1024)}, u32[]{:S(2)}) copy-start(s32[2048]{0:T(1024)} %param.10) | copy-start | bytes 24580
  2.1 0.7 %copy-start.4 = (s32[2,512]{1,0:T(2,128)S(1)}, s32[2,512]{1,0:T(2,128)}, u32[]{:S(2)}) copy-start(s32[2,512]{1,0:T(2,128)} %har_ref.1) | copy-start | bytes 12292
  2.7 0.7 %copy-start.5 = (bf16[2,256]{1,0:T(2,128)(2,1)S(1)}, bf16[2,256]{1,0:T(2,128)(2,1)}, u32[]{:S(2)}) copy-start(bf16[2,256]{1,0:T(2,128)(2,1)} %taps_ref.1) | copy-start | bytes 3076

commit v2 on v1

--- a/solution.py
+++ b/solution.py
@@ -38,17 +38,30 @@
 
 def local_kernel(
     fused, n_grp, n_row, blocks, taps_n, width,
-    col_ref, lon_ref, obs_ref, taps_ref, seg_ref, har_ref, *refs,
+    col_in, lon_in, obs_in, taps_in, seg_in, har_in, *refs,
 ):
     if fused:
-        (out_ref, small_ref, design, filt, table, matrix, lab_col, lab, waves, gram,
+        (out_ref, small_ref, col_ref, lon_ref, obs_got, taps_ref, seg_ref, har_ref, in_sem,
+         obs_ref, fresh, window, filt, table, matrix, lab_col, lab, waves, gram,
          halo_send, halo, sa, ra, sb, rb, sc, rc, sd, rd, rs, rr, rz, send_sem, recv_sem) = refs
     else:
-        (halo, gram, small_ref, design, filt, table, matrix, lab_col, lab, waves) = refs
+        (halo, gram, small_ref, col_ref, lon_ref, obs_got, taps_ref, seg_ref, har_ref, in_sem,
+         obs_ref, fresh, window, filt, table, matrix, lab_col, lab, waves) = refs
     per = taps_n // LANES
+    own = blocks * per
     col_tiles = width // LANES
     row_index = lax.axis_index("row")
     grp_index = lax.axis_index("grp")
+
+    fetched = (
+        (har_in, har_ref), (taps_in, taps_ref), (col_in, col_ref.at[0:own]),
+        (lon_in, lon_ref.at[0:own]), (seg_in, seg_ref), (obs_in, obs_got),
+    )
+    fetches = [
+        pltpu.make_async_copy(src, dst, in_sem.at[k]) for k, (src, dst) in enumerate(fetched)
+    ]
+    for fetch in fetches:
+        fetch.start()
 
     if fused:
         core = lax.rem(row_index, 2)
@@ -66,7 +79,6 @@
         barrier = pltpu.get_barrier_semaphore()
         for peer in greeted:
             pl.semaphore_signal(barrier, inc=1, device_id=peer, device_id_type=pl.DeviceIdType.MESH)
-        pl.semaphore_wait(barrier, len(greeted))
 
         def copy(src, dst, number, peer):
             c = pltpu.make_async_remote_copy(
@@ -77,7 +89,12 @@
             c.start()
             return c
 
-        last = blocks * per - per
+    for fetch in fetches:
+        fetch.wait()
+    obs_ref[:, 0:own * LANES] = obs_got[...].astype(F32)
+
+    if fused:
+        last = own - per
         halo_send[0:per] = col_ref[last:last + per]
         halo_send[per:2 * per] = lon_ref[last:last + per]
         halo_send[2 * per:3 * per] = seg_ref[last:last + per].astype(F32)
@@ -85,8 +102,9 @@
             for p in range(per):
                 at = (last + p) * LANES
                 halo_send[(3 + c) * per + p:(3 + c) * per + p + 1] = obs_ref[
-                    c:c + 1, at:at + LANES].astype(F32)
+                    c:c + 1, at:at + LANES]
         halo_send[5 * per:] = jnp.zeros((halo_send.shape[0] - 5 * per, LANES), F32)
+        pl.semaphore_wait(barrier, len(greeted))
         halo_copy = copy(halo_send, halo, 0, after)
 
     degree = har_ref[0:1, :].astype(F32)
@@ -98,6 +116,48 @@
             here = slice(t * LANES, (t + 1) * LANES)
             waves[number, here, :] = jnp.broadcast_to(values[:, here], (LANES, LANES)).T
 
+    below = lax.broadcasted_iota(jnp.int32, (EXTRA, LANES), 0) == 0
+
+    def design_block(slot):
+        for half in range(per):
+            tile = slot * per + half
+            lanes = slice(half * LANES, (half + 1) * LANES)
+            theta_high, theta_low = turns(col_ref[pl.ds(tile, 1), :])
+            phi_high, phi_low = turns(lon_ref[pl.ds(tile, 1), :])
+            for chunk in range(width // CHUNK):
+                rows = slice(chunk * CHUNK, (chunk + 1) * CHUNK)
+                n = waves[0, rows, :]
+                m = waves[1, rows, :]
+                a = n * theta_high
+                a = (a - jnp.round(a)) + n * theta_low
+                b = m * phi_high + waves[2, rows, :]
+                b = (b - jnp.round(b)) + m * phi_low
+                ua = a * a
+                ub = b * b
+                sin_a = a * poly(ua, SIN_C)
+                cos_a = poly(ua, COS_C)
+                sin_b = b * poly(ub, SIN_C)
+                w = 1.0 - sin_b * sin_b
+                fresh[0, rows, lanes] = ((1.0 - sin_a * sin_a) * w).astype(BF16)
+                fresh[1, rows, lanes] = ((sin_a * cos_a) * w).astype(BF16)
+            at = pl.multiple_of(tile * LANES, LANES)
+            for c in range(2):
+                values = obs_ref[c:c + 1, pl.ds(at, LANES)]
+                fresh[c, width:, lanes] = jnp.where(
+                    below, jnp.broadcast_to(values, (EXTRA, LANES)), 0.0
+                ).astype(BF16)
+
+    def shift():
+        window[:, :, taps_n:] = window[:, :, :taps_n]
+        window[:, :, :taps_n] = fresh[...]
+
+    window[:, :, :taps_n] = jnp.zeros((2, width + EXTRA, taps_n), BF16)
+
+    @pl.loop(0, 2)
+    def _(step):
+        design_block(blocks - 1 - step)
+        shift()
+
     j = lax.broadcasted_iota(jnp.int32, (taps_n, taps_n), 0)
     i = lax.broadcasted_iota(jnp.int32, (taps_n, taps_n), 1)
     for c in range(2):
@@ -110,117 +170,84 @@
         lax.broadcasted_iota(jnp.int32, (LANES, LANES), 0)
         <= lax.broadcasted_iota(jnp.int32, (LANES, LANES), 1)
     ).astype(BF16)
-    within = jnp.dot(seg_ref[...].astype(F32).astype(BF16), upper, preferred_element_type=F32)
-    offset = jnp.zeros((1, 1), F32)
-    for r in range(blocks * per):
-        lab[per + r:per + r + 1, :] = within[r:r + 1] + offset
-        offset = offset + within[r:r + 1, LANES - 1:]
-
-    def label_columns(tile):
+
+    def running(flags, count):
+        within = jnp.dot(flags.astype(BF16), upper, preferred_element_type=F32)
+        offset = jnp.zeros((1, 1), F32)
+        rows = []
+        for r in range(count):
+            rows.append(within[r:r + 1] + offset)
+            offset = offset + within[r:r + 1, LANES - 1:]
+        return rows, offset
+
+    rows, _ = running(seg_ref[...].astype(F32), own)
+    for r in range(own):
+        lab[r:r + 1, :] = rows[r]
+    if fused:
+        halo_copy.wait()
+    rows, total = running(halo[2 * per:3 * per], per)
+    first = row_index == 0
+    for r in range(per):
+        lab[own + r:own + r + 1, :] = jnp.where(first, -1.0, rows[r] - total)
+        for c in range(2):
+            at = (3 + c) * per + r
+            obs_ref[c:c + 1, (own + r) * LANES:(own + r + 1) * LANES] = halo[at:at + 1]
+    col_ref[own:own + per] = halo[0:per]
+    lon_ref[own:own + per] = halo[per:2 * per]
+
+    @pl.loop(0, own + per)
+    def _(tile):
         at = pl.multiple_of(tile * LANES, LANES)
         lab_col[pl.ds(at, LANES), :] = jnp.broadcast_to(lab[pl.ds(tile, 1), :], (LANES, LANES)).T
 
-    @pl.loop(per, (blocks + 1) * per)
-    def _(tile):
-        label_columns(tile)
-
-    def design_tile(theta, phi, tile):
-        at = pl.multiple_of(tile * LANES, LANES)
-        theta_high, theta_low = turns(theta)
-        phi_high, phi_low = turns(phi)
-
-        @pl.loop(0, width // CHUNK)
-        def _(chunk):
-            rows = pl.ds(pl.multiple_of(chunk * CHUNK, CHUNK), CHUNK)
-            n = waves[0, rows, :]
-            m = waves[1, rows, :]
-            a = n * theta_high
-            a = (a - jnp.round(a)) + n * theta_low
-            b = m * phi_high + waves[2, rows, :]
-            b = (b - jnp.round(b)) + m * phi_low
-            ua = a * a
-            ub = b * b
-            sin_a = a * poly(ua, SIN_C)
-            cos_a = poly(ua, COS_C)
-            sin_b = b * poly(ub, SIN_C)
-            w = 1.0 - sin_b * sin_b
-            design[0, rows, pl.ds(at, LANES)] = ((1.0 - sin_a * sin_a) * w).astype(BF16)
-            design[1, rows, pl.ds(at, LANES)] = ((sin_a * cos_a) * w).astype(BF16)
-
-    below = lax.broadcasted_iota(jnp.int32, (EXTRA, LANES), 0) == 0
-
-    def signal_tile(values, c, tile):
-        at = pl.multiple_of(tile * LANES, LANES)
-        design[c, width:, pl.ds(at, LANES)] = jnp.where(
-            below, jnp.broadcast_to(values, (EXTRA, LANES)), 0.0
-        ).astype(BF16)
-
-    @pl.loop(0, blocks * per)
-    def _(tile):
-        design_tile(col_ref[pl.ds(tile, 1), :], lon_ref[pl.ds(tile, 1), :], tile + per)
-        for c in range(2):
-            at = pl.multiple_of(tile * LANES, LANES)
-            signal_tile(obs_ref[c:c + 1, pl.ds(at, LANES)].astype(F32), c, tile + per)
-
-    if fused:
-        halo_copy.wait()
-    counts = jnp.dot(
-        halo[2 * per:3 * per].astype(BF16), upper, preferred_element_type=F32
-    )
-    offset = jnp.zeros((1, 1), F32)
-    rows = []
-    for r in range(per):
-        rows.append(counts[r:r + 1] + offset)
-        offset = offset + counts[r:r + 1, LANES - 1:]
-    first = row_index == 0
-    for r in range(per):
-        lab[r:r + 1, :] = jnp.where(first, -1.0, rows[r] - offset)
-        label_columns(r)
-
-    @pl.loop(0, per)
-    def _(tile):
-        design_tile(halo[pl.ds(tile, 1), :], halo[pl.ds(per + tile, 1), :], tile)
-        for c in range(2):
-            signal_tile(halo[pl.ds((3 + c) * per + tile, 1), :], c, tile)
-
-    epochs = blocks * taps_n
-
-    @pl.loop(0, blocks)
-    def _(block):
-        window = pl.multiple_of(block * taps_n, taps_n)
+    half_width = width // 2
+    half_tiles = half_width // LANES
+    gram[...] = jnp.zeros(gram.shape, F32)
+
+    def filter_block(block):
+        slots = (lax.rem(block + blocks, blocks + 1), block)
         for half in range(per):
             lanes = slice(half * LANES, (half + 1) * LANES)
-            out_label = lab[pl.ds((block + 1) * per + half, 1), :]
-            for part in range(2 * taps_n // LANES):
+            out_label = lab[pl.ds(block * per + half, 1), :]
+            for part in range(2 * per):
                 at = slice(part * LANES, (part + 1) * LANES)
-                same = lab_col[pl.ds(window + part * LANES, LANES), :] == out_label
+                tile = slots[part // per] * per + part % per
+                got = lab_col[pl.ds(pl.multiple_of(tile * LANES, LANES), LANES), :]
+                same = got == out_label
                 for c in range(2):
                     matrix[c, at, lanes] = jnp.where(same, table[c, at, lanes], 0.0).astype(BF16)
         for c in range(2):
-            filt[:, pl.ds(pl.multiple_of(c * epochs + window, taps_n), taps_n)] = jnp.dot(
-                design[c, :, pl.ds(window, 2 * taps_n)], matrix[c],
-                preferred_element_type=F32,
+            filt[:, c * taps_n:(c + 1) * taps_n] = jnp.dot(
+                window[c], matrix[c], preferred_element_type=F32
             ).astype(BF16)
 
-    half_width = width // 2
-    half_tiles = half_width // LANES
-    depth = min(1024, 2 * epochs)
+    def gram_half(half):
+        from_row = half * half_width
+        part = lax.dot_general(
+            filt[from_row:, :], filt[from_row:from_row + half_width, :],
+            (((1,), (1,)), ((), ())), preferred_element_type=F32,
+        )
+        for t in range(half_tiles):
+            gram[half * half_tiles + t, from_row:, :] += part[:, t * LANES:(t + 1) * LANES]
+
+    @pl.loop(0, blocks - 1)
+    def _(step):
+        block = blocks - 1 - step
+        design_block(lax.rem(block - 2 + blocks + 1, blocks + 1))
+        filter_block(block)
+        gram_half(0)
+        gram_half(1)
+        shift()
+
+    filter_block(0)
     copies_a = []
     for half in range(2):
-        gram[half * half_tiles:(half + 1) * half_tiles] = jnp.zeros(
-            (half_tiles, width + EXTRA, LANES), F32
-        )
-
-        @pl.loop(0, 2 * epochs // depth)
-        def _(step):
-            at = pl.ds(pl.multiple_of(step * depth, depth), depth)
-            part = lax.dot_general(
-                filt[:, at], filt[half * half_width:(half + 1) * half_width, at],
-                (((1,), (1,)), ((), ())), preferred_element_type=F32,
-            )
+        gram_half(half)
+        if half == 1:
             for t in range(half_tiles):
-                gram[half * half_tiles + t] += part[:, t * LANES:(t + 1) * LANES]
-
+                for q in range(half_tiles):
+                    gram[half_tiles + t, q * LANES:(q + 1) * LANES, :] = gram[
+                        q, half_width + t * LANES:half_width + (t + 1) * LANES, :].T
         if fused:
             tile_rows = width // n_row
             for t in range(half * half_tiles, (half + 1) * half_tiles):
@@ -328,8 +355,17 @@
     inputs = [split[0], split[1], observed, filter_taps, split[2], harmonic]
     window = rows_here + taps_n
     scratch = [
-        pltpu.VMEM((2, width + EXTRA, window), BF16),
-        pltpu.VMEM((width + EXTRA, 2 * rows_here), BF16),
+        pltpu.VMEM((window // LANES, LANES), F32),
+        pltpu.VMEM((window // LANES, LANES), F32),
+        pltpu.VMEM(observed.shape, observed.dtype),
+        pltpu.VMEM(filter_taps.shape, filter_taps.dtype),
+        pltpu.VMEM((rows_here // LANES, LANES), segment_start.dtype),
+        pltpu.VMEM(harmonic.shape, harmonic.dtype),
+        pltpu.SemaphoreType.DMA((6,)),
+        pltpu.VMEM((2, window), F32),
+        pltpu.VMEM((2, width + EXTRA, taps_n), BF16),
+        pltpu.VMEM((2, width + EXTRA, 2 * taps_n), BF16),
+        pltpu.VMEM((width + EXTRA, 2 * taps_n), BF16),
         pltpu.VMEM((2, 2 * taps_n, taps_n), F32),
         pltpu.VMEM((2, 2 * taps_n, taps_n), BF16),
         pltpu.VMEM((window, LANES), F32),
@@ -371,13 +407,14 @@
         pairs = [(k, k + 1) for k in range(n_row - 1)]
         inputs.append(lax.ppermute(jnp.concatenate(pieces), "row", pairs))
         main_shape = jax.ShapeDtypeStruct(gram_shape, F32)
-    params = dict(vmem_limit_bytes=40 * 1024 * 1024)
+    params = dict(vmem_limit_bytes=48 * 1024 * 1024)
     if fused:
         params.update(collective_id=0, has_side_effects=True)
     main, small = pl.pallas_call(
         functools.partial(local_kernel, fused, n_grp, n_row, blocks, taps_n, width),
         out_shape=(main_shape, small_shape),
-        in_specs=[pl.BlockSpec(memory_space=pltpu.VMEM)] * len(inputs),
+        in_specs=[pl.BlockSpec(memory_space=pltpu.HBM)] * 6
+        + [pl.BlockSpec(memory_space=pltpu.VMEM)] * (len(inputs) - 6),
         out_specs=(pl.BlockSpec(memory_space=pltpu.VMEM),) * 2,
         scratch_shapes=scratch,
         compiler_params=pltpu.CompilerParams(**params),

time: 40.5 us -> 38.3 us (0.946)
  Pallas kernels: 35.4 us -> 33.2 us
    pallas_call x1, Pallas kernels: 35.4 us -> 33.2 us  [on_device(): pl.pallas_call(functools.partial(local_kernel, fused, n_grp, n_row, block...]
where the time goes in v2:
time: 38.3 us; the launch traced here: 37.9 us
  Pallas kernels  33.2 us (87%)
  local copies, waits for them, and re-layouts  2.74 us (7%)
  other arithmetic  1.29 us (3%)
  between operations  0.69 us (2%)
    pallas_call x1, Pallas kernels, on_device(): pl.pallas_call(functools.partial(local_kernel, fused, n_grp, n_row, block...  33.2 us
    unnamed x12, local copies, waits for them, and re-layouts  2.74 us

profile of v2, /device:TPU:0, one launch (start us, length us, event | category | flops | bytes accessed | tf_op | source)
XLA Modules:
  0.0 37.9 jit_solution(7538491348038515499)
XLA Ops:
  0.6 0.0 copy-start.2
  0.6 0.0 copy-start.1
  0.7 0.0 copy-start
  0.7 0.6 %copy-done.2 = bf16[2,2048]{1,0:T(2,128)(2,1)S(1)} copy-done((bf16[2,2048]{1,0:T(2,128)(2,1)S(1)}, bf16[2,2048]{1,0:T(2,128)(2,1)}, u32[]{:S(2)}) %copy-start.2) | copy-done | bytes 8216
  1.3 0.0 copy-done.1
  1.3 0.0 copy-done
  1.4 0.0 copy-start.3
  1.4 0.7 %copy-done.3 = s32[2048]{0:T(1024)S(1)} copy-done((s32[2048]{0:T(1024)S(1)}, s32[2048]{0:T(1024)}, u32[]{:S(2)}) %copy-start.3) | copy-done | bytes 8216
  2.1 0.0 copy-start.4
  2.1 0.7 %copy-done.4 = s32[2,512]{1,0:T(2,128)S(1)} copy-done((s32[2,512]{1,0:T(2,128)S(1)}, s32[2,512]{1,0:T(2,128)}, u32[]{:S(2)}) %copy-start.4) | copy-done | bytes 4120
  2.7 0.0 copy-start.5
  2.7 0.7 %copy-done.5 = bf16[2,256]{1,0:T(2,128)(2,1)S(1)} copy-done((bf16[2,256]{1,0:T(2,128)(2,1)S(1)}, bf16[2,256]{1,0:T(2,128)(2,1)}, u32[]{:S(2)}) %copy-start.5) | copy-done | bytes 1048
  3.4 33.2 %normal_equations.1 = (f32[64,128]{1,0:T(8,128)S(1)}, f32[8,128]{1,0:T(8,128)S(1)}) custom-call(f32[16,128]{1,0:T(8,128)S(1)} %bitcast.7, f32[16,128]{1,0:T(8,128)S(1)} %bitcast.8, bf16[2,2048]{1,0:T(2,128)(2,1)S(1)} %copy-done.2, bf16[2,256]{1,0:T(2,128)(2,1)S(1)} %copy-done.5, s32[16,128]{1,0:T(8,128)S(1)} %bitcast.9, s32[2,512]{1,0:T(2,128)S(1)} %copy-done.4), custom_call_target="tpu_custom_call" | custom-call | tf_op jit(solution)/shard_map/normal_equations/pallas_call | solution.py:413
  36.6 0.7 %multiply_select_fusion = f32[64,128]{1,0:T(8,128)} fusion(f32[64,128]{1,0:T(8,128)S(1)} %get-tuple-element.5, s32[128]{0:T(128)S(1)} %iota_add_fusion, s32[64]{0:T(128)S(1)} %iota_add_fusion.1), kind=kLoop, calls=%fused_computation | loop fusion | flops 24576 | bytes 66304 | tf_op jit(solution)/shard_map/jit(_where)/select_n | solution.py:436
  37.3 0.6 %multiply_bitcast_fusion = (f32[512]{0:T(512)}, f32[512]{0:T(512)}) fusion(f32[8,128]{1,0:T(8,128)S(1)} %get-tuple-element.6), kind=kLoop, calls=%fused_computation.1 | loop fusion | flops 1024 | bytes 8192 | tf_op jit(solution)/shard_map/mul | solution.py:438
  (2 shorter events, 0.0 us)
Async XLA Ops:
  0.6 0.7 %copy-start.2 = (bf16[2,2048]{1,0:T(2,128)(2,1)S(1)}, bf16[2,2048]{1,0:T(2,128)(2,1)}, u32[]{:S(2)}) copy-start(bf16[2,2048]{1,0:T(2,128)(2,1)} %obs_in.1) | copy-start | bytes 24580
  0.6 0.7 %copy-start.1 = (f32[2048]{0:T(1024)S(1)}, f32[2048]{0:T(1024)}, u32[]{:S(2)}) copy-start(f32[2048]{0:T(1024)} %param.7) | copy-start | bytes 24580
  0.7 0.7 %copy-start = (f32[2048]{0:T(1024)S(1)}, f32[2048]{0:T(1024)}, u32[]{:S(2)}) copy-start(f32[2048]{0:T(1024)} %param.6) | copy-start | bytes 24580
  1.4 0.7 %copy-start.3 = (s32[2048]{0:T(1024)S(1)}, s32[2048]{0:T(1024)}, u32[]{:S(2)}) copy-start(s32[2048]{0:T(1024)} %param.10) | copy-start | bytes 24580
  2.1 0.7 %copy-start.4 = (s32[2,512]{1,0:T(2,128)S(1)}, s32[2,512]{1,0:T(2,128)}, u32[]{:S(2)}) copy-start(s32[2,512]{1,0:T(2,128)} %har_in.1) | copy-start | bytes 12292
  2.7 0.7 %copy-start.5 = (bf16[2,256]{1,0:T(2,128)(2,1)S(1)}, bf16[2,256]{1,0:T(2,128)(2,1)}, u32[]{:S(2)}) copy-start(bf16[2,256]{1,0:T(2,128)(2,1)} %taps_in.1) | copy-start | bytes 3076

commit v3 on v2

--- a/solution.py
+++ b/solution.py
@@ -27,26 +27,34 @@
     return total
 
 
+def nearest(x):
+    return (x + 12582912.0) - 12582912.0
+
+
+def spread(columns, k):
+    return jnp.broadcast_to(columns[:, k:k + 1], (LANES, LANES))
+
+
 def turns(angle):
-    head = jnp.round(angle * 1024.0) * (1.0 / 1024.0)
+    head = nearest(angle * 1024.0) * (1.0 / 1024.0)
     tail = angle - head
     coarse = head * TURN_HIGH
-    high = jnp.round(coarse * 32768.0) * (1.0 / 32768.0)
+    high = nearest(coarse * 32768.0) * (1.0 / 32768.0)
     low = (coarse - high) + (head * TURN_LOW + tail * (TURN_HIGH + TURN_LOW))
     return high, low
 
 
 def local_kernel(
-    fused, n_grp, n_row, blocks, taps_n, width,
+    fused, n_grp, n_row, blocks, taps_n, width, gram_scale, row_scale,
     col_in, lon_in, obs_in, taps_in, seg_in, har_in, *refs,
 ):
     if fused:
         (out_ref, small_ref, col_ref, lon_ref, obs_got, taps_ref, seg_ref, har_ref, in_sem,
-         obs_ref, fresh, window, filt, table, matrix, lab_col, lab, waves, gram,
+         obs_ref, fresh, window, filt, table, matrix, lab_col, lab, waves, turned, gram,
          halo_send, halo, sa, ra, sb, rb, sc, rc, sd, rd, rs, rr, rz, send_sem, recv_sem) = refs
     else:
         (halo, gram, small_ref, col_ref, lon_ref, obs_got, taps_ref, seg_ref, har_ref, in_sem,
-         obs_ref, fresh, window, filt, table, matrix, lab_col, lab, waves) = refs
+         obs_ref, fresh, window, filt, table, matrix, lab_col, lab, waves, turned) = refs
     per = taps_n // LANES
     own = blocks * per
     col_tiles = width // LANES
@@ -111,10 +119,16 @@
     order = har_ref[1:2, :]
     size = jnp.abs(order).astype(F32)
     phase = jnp.where(order >= 0, 0.0, -0.25).astype(F32)
-    for number, values in enumerate((degree, size, phase)):
+    turned[...] = jnp.zeros((LANES, LANES), F32)
+    number = 0
+    for values in (degree, size, phase):
         for t in range(col_tiles):
-            here = slice(t * LANES, (t + 1) * LANES)
-            waves[number, here, :] = jnp.broadcast_to(values[:, here], (LANES, LANES)).T
+            turned[number:number + 1, :] = values[:, t * LANES:(t + 1) * LANES]
+            number += 1
+    columns = turned[...].T
+    for number in range(3):
+        for t in range(col_tiles):
+            waves[number, t * LANES:(t + 1) * LANES, :] = spread(columns, number * col_tiles + t)
 
     below = lax.broadcasted_iota(jnp.int32, (EXTRA, LANES), 0) == 0
 
@@ -129,9 +143,9 @@
                 n = waves[0, rows, :]
                 m = waves[1, rows, :]
                 a = n * theta_high
-                a = (a - jnp.round(a)) + n * theta_low
+                a = (a - nearest(a)) + n * theta_low
                 b = m * phi_high + waves[2, rows, :]
-                b = (b - jnp.round(b)) + m * phi_low
+                b = (b - nearest(b)) + m * phi_low
                 ua = a * a
                 ub = b * b
                 sin_a = a * poly(ua, SIN_C)
@@ -161,44 +175,46 @@
     j = lax.broadcasted_iota(jnp.int32, (taps_n, taps_n), 0)
     i = lax.broadcasted_iota(jnp.int32, (taps_n, taps_n), 1)
     for c in range(2):
-        row = jnp.broadcast_to(taps_ref[c:c + 1, :].astype(F32), (taps_n, taps_n))
-        around = pltpu.roll(row, 0, 1, stride=1, stride_axis=0)
-        table[c, 0:taps_n, :] = jnp.where(i < j, around, 0.0)
-        table[c, taps_n:, :] = jnp.where(i >= j, around, 0.0)
-
-    upper = (
-        lax.broadcasted_iota(jnp.int32, (LANES, LANES), 0)
-        <= lax.broadcasted_iota(jnp.int32, (LANES, LANES), 1)
-    ).astype(BF16)
-
-    def running(flags, count):
-        within = jnp.dot(flags.astype(BF16), upper, preferred_element_type=F32)
-        offset = jnp.zeros((1, 1), F32)
-        rows = []
-        for r in range(count):
-            rows.append(within[r:r + 1] + offset)
-            offset = offset + within[r:r + 1, LANES - 1:]
-        return rows, offset
-
-    rows, _ = running(seg_ref[...].astype(F32), own)
-    for r in range(own):
-        lab[r:r + 1, :] = rows[r]
+        row = jnp.broadcast_to(taps_ref[c:c + 1, :].astype(F32), (8, taps_n))
+        base = pltpu.roll(row, 0, 1, stride=1, stride_axis=0)
+        for r in range(0, taps_n, 8):
+            around = pltpu.roll(base, r, 1) if r else base
+            early = i[r:r + 8] < j[r:r + 8]
+            table[c, r:r + 8, :] = jnp.where(early, around, 0.0)
+            table[c, taps_n + r:taps_n + r + 8, :] = jnp.where(early, 0.0, around)
+
+    first_lane = lax.broadcasted_iota(jnp.int32, (LANES, LANES), 0)
+    second_lane = lax.broadcasted_iota(jnp.int32, (LANES, LANES), 1)
+    ones = jnp.ones((LANES, LANES), BF16)
+
+    def counted(flags, lanes, rows):
+        here = jnp.dot(flags, lanes.astype(BF16), preferred_element_type=F32)
+        others = jnp.dot(rows.astype(BF16), flags, preferred_element_type=F32)
+        return here + jnp.dot(others.astype(BF16), ones, preferred_element_type=F32)
+
+    first_row = lax.broadcasted_iota(jnp.int32, (own, own), 0)
+    second_row = lax.broadcasted_iota(jnp.int32, (own, own), 1)
+    lab[0:own] = counted(
+        seg_ref[...].astype(F32).astype(BF16), first_lane <= second_lane, second_row < first_row
+    )
     if fused:
         halo_copy.wait()
-    rows, total = running(halo[2 * per:3 * per], per)
+    first_row = lax.broadcasted_iota(jnp.int32, (halo.shape[0], halo.shape[0]), 0)
+    second_row = lax.broadcasted_iota(jnp.int32, (halo.shape[0], halo.shape[0]), 1)
+    later = (first_row < second_row) & (second_row < 3 * per)
+    ahead = counted(halo[...].astype(BF16), first_lane > second_lane, later)
     first = row_index == 0
+    lab[own:own + per] = jnp.where(first, -1.0, -ahead[2 * per:3 * per])
     for r in range(per):
-        lab[own + r:own + r + 1, :] = jnp.where(first, -1.0, rows[r] - total)
         for c in range(2):
             at = (3 + c) * per + r
             obs_ref[c:c + 1, (own + r) * LANES:(own + r + 1) * LANES] = halo[at:at + 1]
     col_ref[own:own + per] = halo[0:per]
     lon_ref[own:own + per] = halo[per:2 * per]
-
-    @pl.loop(0, own + per)
-    def _(tile):
-        at = pl.multiple_of(tile * LANES, LANES)
-        lab_col[pl.ds(at, LANES), :] = jnp.broadcast_to(lab[pl.ds(tile, 1), :], (LANES, LANES)).T
+    turned[0:own + per] = lab[...]
+    columns = turned[...].T
+    for tile in range(own + per):
+        lab_col[tile * LANES:(tile + 1) * LANES, :] = spread(columns, tile)
 
     half_width = width // 2
     half_tiles = half_width // LANES
@@ -329,13 +345,16 @@
     for k in range(1, n_z):
         copies_d[k - 1].wait()
         total = total + rd[k - 1].astype(F32)
-    out_ref[...] = total
+    row_at = row_index * tile_rows + lax.broadcasted_iota(jnp.int32, total.shape, 0)
+    col_at = grp_index * LANES + lax.broadcasted_iota(jnp.int32, total.shape, 1)
+    out_ref[...] = jnp.where(row_at == col_at, 0.0, total * gram_scale)
     for c in small_d:
         c.wait()
     total = rz[0]
     for zz in range(1, n_z):
         total = total + rz[zz]
-    small_ref[...] = total
+    small_ref[0:col_tiles] = total[0:col_tiles] * gram_scale
+    small_ref[col_tiles:] = total[col_tiles:] * row_scale
 
 
 def on_device(colatitude, longitude, observed, filter_taps, segment_start, harmonic):
@@ -371,6 +390,7 @@
         pltpu.VMEM((window, LANES), F32),
         pltpu.VMEM((window // LANES, LANES), F32),
         pltpu.VMEM((3, width, LANES), F32),
+        pltpu.VMEM((LANES, LANES), F32),
     ]
     gram_shape = (tiles, width + EXTRA, LANES)
     small_shape = jax.ShapeDtypeStruct((2 * tiles, LANES), F32)
@@ -407,11 +427,13 @@
         pairs = [(k, k + 1) for k in range(n_row - 1)]
         inputs.append(lax.ppermute(jnp.concatenate(pieces), "row", pairs))
         main_shape = jax.ShapeDtypeStruct(gram_shape, F32)
-    params = dict(vmem_limit_bytes=48 * 1024 * 1024)
+    params = dict(vmem_limit_bytes=64 * 1024 * 1024)
     if fused:
         params.update(collective_id=0, has_side_effects=True)
     main, small = pl.pallas_call(
-        functools.partial(local_kernel, fused, n_grp, n_row, blocks, taps_n, width),
+        functools.partial(
+            local_kernel, fused, n_grp, n_row, blocks, taps_n, width, gram_scale, row_scale
+        ),
         out_shape=(main_shape, small_shape),
         in_specs=[pl.BlockSpec(memory_space=pltpu.HBM)] * 6
         + [pl.BlockSpec(memory_space=pltpu.VMEM)] * (len(inputs) - 6),
@@ -421,12 +443,11 @@
         name="normal_equations",
     )(*inputs)
     if fused:
-        normal = main
-    else:
-        gram = main[:, :width].transpose(1, 0, 2).reshape(width, width)
-        owned = lax.psum_scatter(gram, "row", scatter_dimension=0, tiled=True)
-        normal = lax.psum_scatter(owned, "grp", scatter_dimension=1, tiled=True)
-        small = lax.psum(small, ("grp", "row"))
+        return (main, small[:tiles].reshape(width), small[tiles:].reshape(width))
+    gram = main[:, :width].transpose(1, 0, 2).reshape(width, width)
+    owned = lax.psum_scatter(gram, "row", scatter_dimension=0, tiled=True)
+    normal = lax.psum_scatter(owned, "grp", scatter_dimension=1, tiled=True)
+    small = lax.psum(small, ("grp", "row"))
     row_at = lax.axis_index("row") * normal.shape[0] + lax.broadcasted_iota(
         jnp.int32, normal.shape, 0
     )

time: 38.3 us -> 36.7 us (0.958)
  other arithmetic: 1.29 us -> 0 us
    unnamed x12 -> x1, local copies, waits for them, and re-layouts: 2.74 us -> 1.37 us
    reshape x0 -> x1, local copies, waits for them, and re-layouts: none -> 1.34 us  [on_device(): return (main, small[:tiles].reshape(width), small[tiles:].reshape(width))]
    select_n x1 -> x0, other arithmetic: 0.69 us -> none  [on_device(): normal = jnp.where(row_at == col_at, 0.0, normal * gram_scale)]
    mul x1 -> x0, other arithmetic: 0.58 us -> none  [on_device(): diagonal = small[tiles:].reshape(width) * row_scale]
where the time goes in v3:
time: 36.7 us; the launch traced here: 36.4 us
  Pallas kernels  33 us (90%)
  local copies, waits for them, and re-layouts  2.71 us (7%)
  between operations  0.64 us (2%)
    pallas_call x1, Pallas kernels, on_device(): pl.pallas_call(functools.partial(local_kernel, fused, n_grp, n_row, block...  33 us
    unnamed x1, local copies, waits for them, and re-layouts  1.37 us
    reshape x1, local copies, waits for them, and re-layouts, on_device(): return (main, small[:tiles].reshape(width), small[tiles:].reshape(width))  1.34 us

profile of v3, /device:TPU:0, one launch (start us, length us, event | category | flops | bytes accessed | tf_op | source)
XLA Modules:
  0.0 36.4 jit_solution(471357245545582225)
XLA Ops:
  0.6 33.0 %normal_equations.1 = (f32[64,128]{1,0:T(8,128)}, f32[8,128]{1,0:T(8,128)}) custom-call(f32[16,128]{1,0:T(8,128)} %bitcast.7, f32[16,128]{1,0:T(8,128)} %bitcast.8, bf16[2,2048]{1,0:T(2,128)(2,1)} %obs_in.1, bf16[2,256]{1,0:T(2,128)(2,1)} %taps_in.1, s32[16,128]{1,0:T(8,128)} %bitcast.9, s32[2,512]{1,0:T(2,128)} %har_in.1), custom_call_target="tpu_custom_call" | custom-call | tf_op jit(solution)/shard_map/normal_equations/pallas_call | solution.py:433
  33.6 1.3 %slice_bitcast_fusion = (f32[512]{0:T(512)}, f32[512]{0:T(512)}) fusion(f32[8,128]{1,0:T(8,128)} %get-tuple-element.6), kind=kLoop, calls=%fused_computation | loop fusion | bytes 8192 | tf_op jit(solution)/shard_map/reshape | solution.py:446
  35.0 1.4 %copy.10 = f32[64,128]{1,0:T(8,128)} copy(f32[64,128]{1,0:T(8,128)} %get-tuple-element.12) | data formatting | bytes 65536

commit v4 on v3

--- a/solution.py
+++ b/solution.py
@@ -17,6 +17,7 @@
 COS_C = (1.41420316696167, -6.977553367614746, 5.714066982269287, -1.7246402502059937)
 TURN_HIGH = 2608.0 / 16384.0
 TURN_LOW = 1.0 / (2.0 * math.pi) - TURN_HIGH
+TURN_UNIT = 2.0**-32
 FUSED = True
 
 
@@ -39,9 +40,21 @@
     head = nearest(angle * 1024.0) * (1.0 / 1024.0)
     tail = angle - head
     coarse = head * TURN_HIGH
-    high = nearest(coarse * 32768.0) * (1.0 / 32768.0)
-    low = (coarse - high) + (head * TURN_LOW + tail * (TURN_HIGH + TURN_LOW))
-    return high, low
+    high = nearest(coarse * 32768.0)
+    low = (coarse - high * (1.0 / 32768.0)) + (head * TURN_LOW + tail * (TURN_HIGH + TURN_LOW))
+    fine = nearest(low * 2.0**32)
+    return high.astype(jnp.int32) * 131072 + fine.astype(jnp.int32)
+
+
+def hand_on_kernel(*refs):
+    count = (len(refs) - 1) // 2
+    copies = [
+        pltpu.make_async_copy(refs[k], refs[count + k], refs[-1].at[k]) for k in range(count)
+    ]
+    for c in copies:
+        c.start()
+    for c in copies:
+        c.wait()
 
 
 def local_kernel(
@@ -49,7 +62,7 @@
     col_in, lon_in, obs_in, taps_in, seg_in, har_in, *refs,
 ):
     if fused:
-        (out_ref, small_ref, col_ref, lon_ref, obs_got, taps_ref, seg_ref, har_ref, in_sem,
+        (out_ref, right_ref, diag_ref, col_ref, lon_ref, obs_got, taps_ref, seg_ref, har_ref, in_sem,
          obs_ref, fresh, window, filt, table, matrix, lab_col, lab, waves, turned, gram,
          halo_send, halo, sa, ra, sb, rb, sc, rc, sd, rd, rs, rr, rz, send_sem, recv_sem) = refs
     else:
@@ -112,13 +125,11 @@
                 halo_send[(3 + c) * per + p:(3 + c) * per + p + 1] = obs_ref[
                     c:c + 1, at:at + LANES]
         halo_send[5 * per:] = jnp.zeros((halo_send.shape[0] - 5 * per, LANES), F32)
-        pl.semaphore_wait(barrier, len(greeted))
-        halo_copy = copy(halo_send, halo, 0, after)
 
     degree = har_ref[0:1, :].astype(F32)
     order = har_ref[1:2, :]
     size = jnp.abs(order).astype(F32)
-    phase = jnp.where(order >= 0, 0.0, -0.25).astype(F32)
+    phase = jnp.where(order >= 0, 0.0, -1.0).astype(F32)
     turned[...] = jnp.zeros((LANES, LANES), F32)
     number = 0
     for values in (degree, size, phase):
@@ -128,7 +139,10 @@
     columns = turned[...].T
     for number in range(3):
         for t in range(col_tiles):
-            waves[number, t * LANES:(t + 1) * LANES, :] = spread(columns, number * col_tiles + t)
+            unit = 1 << 30 if number == 2 else 1
+            waves[number, t * LANES:(t + 1) * LANES, :] = (
+                spread(columns, number * col_tiles + t).astype(jnp.int32) * unit
+            )
 
     below = lax.broadcasted_iota(jnp.int32, (EXTRA, LANES), 0) == 0
 
@@ -136,24 +150,21 @@
         for half in range(per):
             tile = slot * per + half
             lanes = slice(half * LANES, (half + 1) * LANES)
-            theta_high, theta_low = turns(col_ref[pl.ds(tile, 1), :])
-            phi_high, phi_low = turns(lon_ref[pl.ds(tile, 1), :])
+            theta = turns(col_ref[pl.ds(tile, 1), :])
+            phi = turns(lon_ref[pl.ds(tile, 1), :])
             for chunk in range(width // CHUNK):
                 rows = slice(chunk * CHUNK, (chunk + 1) * CHUNK)
-                n = waves[0, rows, :]
-                m = waves[1, rows, :]
-                a = n * theta_high
-                a = (a - nearest(a)) + n * theta_low
-                b = m * phi_high + waves[2, rows, :]
-                b = (b - nearest(b)) + m * phi_low
+                a = (waves[0, rows, :] * theta).astype(F32) * TURN_UNIT
+                b = (waves[1, rows, :] * phi + waves[2, rows, :]).astype(F32) * TURN_UNIT
                 ua = a * a
                 ub = b * b
                 sin_a = a * poly(ua, SIN_C)
                 cos_a = poly(ua, COS_C)
                 sin_b = b * poly(ub, SIN_C)
                 w = 1.0 - sin_b * sin_b
-                fresh[0, rows, lanes] = ((1.0 - sin_a * sin_a) * w).astype(BF16)
-                fresh[1, rows, lanes] = ((sin_a * cos_a) * w).astype(BF16)
+                sin_w = sin_a * w
+                fresh[0, rows, lanes] = (w - sin_a * sin_w).astype(BF16)
+                fresh[1, rows, lanes] = (cos_a * sin_w).astype(BF16)
             at = pl.multiple_of(tile * LANES, LANES)
             for c in range(2):
                 values = obs_ref[c:c + 1, pl.ds(at, LANES)]
@@ -171,6 +182,10 @@
     def _(step):
         design_block(blocks - 1 - step)
         shift()
+
+    if fused:
+        pl.semaphore_wait(barrier, len(greeted))
+        halo_copy = copy(halo_send, halo, 0, after)
 
     j = lax.broadcasted_iota(jnp.int32, (taps_n, taps_n), 0)
     i = lax.broadcasted_iota(jnp.int32, (taps_n, taps_n), 1)
@@ -353,8 +368,8 @@
     total = rz[0]
     for zz in range(1, n_z):
         total = total + rz[zz]
-    small_ref[0:col_tiles] = total[0:col_tiles] * gram_scale
-    small_ref[col_tiles:] = total[col_tiles:] * row_scale
+    right_ref[...] = total[0:col_tiles] * gram_scale
+    diag_ref[...] = total[col_tiles:] * row_scale
 
 
 def on_device(colatitude, longitude, observed, filter_taps, segment_start, harmonic):
@@ -389,11 +404,11 @@
         pltpu.VMEM((2, 2 * taps_n, taps_n), BF16),
         pltpu.VMEM((window, LANES), F32),
         pltpu.VMEM((window // LANES, LANES), F32),
-        pltpu.VMEM((3, width, LANES), F32),
+        pltpu.VMEM((3, width, LANES), jnp.int32),
         pltpu.VMEM((LANES, LANES), F32),
     ]
     gram_shape = (tiles, width + EXTRA, LANES)
-    small_shape = jax.ShapeDtypeStruct((2 * tiles, LANES), F32)
+    small_shapes = (jax.ShapeDtypeStruct((2 * tiles, LANES), F32),)
     halo_shape = (8 * per, LANES)
     if fused:
         tile_rows = width // n_row
@@ -419,6 +434,7 @@
             pltpu.SemaphoreType.DMA((copies,)),
         ]
         main_shape = jax.ShapeDtypeStruct((tile_rows, LANES), F32)
+        small_shapes = (jax.ShapeDtypeStruct((tiles, LANES), F32),) * 2
     else:
         last = rows_here // LANES - per
         pieces = [split[0][last:], split[1][last:], split[2][last:].astype(F32)]
@@ -430,20 +446,31 @@
     params = dict(vmem_limit_bytes=64 * 1024 * 1024)
     if fused:
         params.update(collective_id=0, has_side_effects=True)
-    main, small = pl.pallas_call(
+    main, *small = pl.pallas_call(
         functools.partial(
             local_kernel, fused, n_grp, n_row, blocks, taps_n, width, gram_scale, row_scale
         ),
-        out_shape=(main_shape, small_shape),
+        out_shape=(main_shape,) + small_shapes,
         in_specs=[pl.BlockSpec(memory_space=pltpu.HBM)] * 6
         + [pl.BlockSpec(memory_space=pltpu.VMEM)] * (len(inputs) - 6),
-        out_specs=(pl.BlockSpec(memory_space=pltpu.VMEM),) * 2,
+        out_specs=(pl.BlockSpec(memory_space=pltpu.VMEM),) * (1 + len(small_shapes)),
         scratch_shapes=scratch,
         compiler_params=pltpu.CompilerParams(**params),
         name="normal_equations",
     )(*inputs)
     if fused:
-        return (main, small[:tiles].reshape(width), small[tiles:].reshape(width))
+        results = (main,) + tuple(small)
+        normal, right_side, diagonal = pl.pallas_call(
+            hand_on_kernel,
+            out_shape=tuple(jax.ShapeDtypeStruct(r.shape, r.dtype) for r in results),
+            in_specs=[pl.BlockSpec(memory_space=pl.ANY)] * 3,
+            out_specs=(pl.BlockSpec(memory_space=pl.ANY),) * 3,
+            scratch_shapes=[pltpu.SemaphoreType.DMA((3,))],
+            compiler_params=pltpu.CompilerParams(vmem_limit_bytes=64 * 1024 * 1024),
+            name="hand_on",
+        )(*results)
+        return (normal, right_side.reshape(width), diagonal.reshape(width))
+    small = small[0]
     gram = main[:, :width].transpose(1, 0, 2).reshape(width, width)
     owned = lax.psum_scatter(gram, "row", scatter_dimension=0, tiled=True)
     normal = lax.psum_scatter(owned, "grp", scatter_dimension=1, tiled=True)

time: 36.7 us -> 35.8 us (0.975)
  local copies, waits for them, and re-layouts: 2.71 us -> 0 us
  Pallas kernels: 33 us -> 35 us
    pallas_call x0 -> x1, Pallas kernels: none -> 2.25 us  [on_device(): pl.pallas_call(hand_on_kernel, out_shape=tuple((jax.ShapeDtypeStruct(r.sh...]
    unnamed x1 -> x0, local copies, waits for them, and re-layouts: 1.37 us -> none
    reshape x1 -> x0, local copies, waits for them, and re-layouts: 1.34 us -> none  [on_device(): return (main, small[:tiles].reshape(width), small[tiles:].reshape(width))]
where the time goes in v4:
time: 35.8 us; the launch traced here: 35.6 us
  Pallas kernels  35 us (98%)
  between operations  0.64 us (2%)
    pallas_call x1, Pallas kernels, on_device(): pl.pallas_call(functools.partial(local_kernel, fused, n_grp, n_row, block...  32.8 us
    pallas_call x1, Pallas kernels, on_device(): pl.pallas_call(hand_on_kernel, out_shape=tuple((jax.ShapeDtypeStruct(r.sh...  2.25 us

profile of v4, /device:TPU:0, one launch (start us, length us, event | category | flops | bytes accessed | tf_op | source)
XLA Modules:
  0.0 35.6 jit_solution(11455843799100978940)
XLA Ops:
  0.6 32.8 %normal_equations.1 = (f32[64,128]{1,0:T(8,128)}, f32[4,128]{1,0:T(4,128)}, f32[4,128]{1,0:T(4,128)}) custom-call(f32[16,128]{1,0:T(8,128)} %bitcast.5, f32[16,128]{1,0:T(8,128)} %bitcast.6, bf16[2,2048]{1,0:T(2,128)(2,1)} %obs_in.1, bf16[2,256]{1,0:T(2,128)(2,1)} %taps_in.1, s32[16,128]{1,0:T(8,128)} %bitcast.7, s32[2,512]{1,0:T(2,128)} %har_in.1), custom_call_target="tpu_custom_call" | custom-call | tf_op jit(solution)/shard_map/normal_equations/pallas_call | solution.py:449
  33.4 2.2 %hand_on.1 = (f32[64,128]{1,0:T(8,128)}, f32[4,128]{1,0:T(4,128)}, f32[4,128]{1,0:T(4,128)}) custom-call(f32[64,128]{1,0:T(8,128)} %get-tuple-element.9.refs_0_, f32[4,128]{1,0:T(4,128)} %get-tuple-element.10.refs_1_, f32[4,128]{1,0:T(4,128)} %get-tuple-element.11.refs_2_), custom_call_target="tpu_custom_call" | custom-call | tf_op jit(solution)/shard_map/hand_on/pallas_call | solution.py:463

commit v5 on v4

--- a/solution.py
+++ b/solution.py
@@ -64,7 +64,7 @@
     if fused:
         (out_ref, right_ref, diag_ref, col_ref, lon_ref, obs_got, taps_ref, seg_ref, har_ref, in_sem,
          obs_ref, fresh, window, filt, table, matrix, lab_col, lab, waves, turned, gram,
-         halo_send, halo, sa, ra, sb, rb, sc, rc, sd, rd, rs, rr, rz, send_sem, recv_sem) = refs
+         halo_send, halo, sa, ra, sb, rb, rs, rr, rx, rz, send_sem, recv_sem) = refs
     else:
         (halo, gram, small_ref, col_ref, lon_ref, obs_got, taps_ref, seg_ref, har_ref, in_sem,
          obs_ref, fresh, window, filt, table, matrix, lab_col, lab, waves, turned) = refs
@@ -87,16 +87,16 @@
     if fused:
         core = lax.rem(row_index, 2)
         z = row_index // 2
-        y = grp_index // 2
-        x = lax.rem(grp_index, 2)
         n_z = n_row // 2
         twin = (grp_index, row_index + 1 - 2 * core)
-        y_peer = (lax.rem(grp_index + 2, 4), row_index)
-        x_peer = (grp_index + 1 - 2 * x, row_index)
+        grp_peers = [(lax.rem(grp_index + k, n_grp), row_index) for k in range(1, n_grp)]
         z_peers = [(grp_index, lax.rem(row_index + 2 * k, n_row)) for k in range(1, n_z)]
         after = (grp_index, lax.rem(row_index + 1, n_row))
         before = (grp_index, lax.rem(row_index + n_row - 1, n_row))
-        greeted = [twin, y_peer, x_peer, after, before] + z_peers
+        greeted = [twin, after, before] + [
+            (lax.rem(grp_index + dg, n_grp), lax.rem(row_index + 2 * dz, n_row))
+            for dg in range(n_grp) for dz in range(n_z) if dg or dz
+        ]
         barrier = pltpu.get_barrier_semaphore()
         for peer in greeted:
             pl.semaphore_signal(barrier, inc=1, device_id=peer, device_id_type=pl.DeviceIdType.MESH)
@@ -316,50 +316,31 @@
     def held(t, zz):
         return gram[t, pl.ds(pl.multiple_of(zz * tile_rows, tile_rows), tile_rows), :]
 
-    def add(t, zz, values):
-        at = pl.ds(pl.multiple_of(zz * tile_rows, tile_rows), tile_rows)
-        gram[t, at, :] = gram[t, at, :] + values.astype(F32)
-
-    z_half = n_z // 2
-    for k in range(2):
-        for q in range(z_half):
-            sb[0, k, q] = held(2 * (1 - y) + k, q).astype(BF16)
-            sb[1, k, q] = held(2 * k + 1 - x, z_half + q).astype(BF16)
-    copies_b = [copy(sb.at[0], rb.at[0], 4, y_peer), copy(sb.at[1], rb.at[1], 5, x_peer)]
     small_a.wait()
-    rs[1] = rs[0] + rr[0]
-    small_b = copy(rs.at[1], rr.at[1], 6, y_peer)
-    copies_b[0].wait()
-    for q in range(z_half):
-        sc[0, q] = (held(2 * y + 1 - x, q) + rb[0, 1 - x, q].astype(F32)).astype(BF16)
-    copies_c = [copy(sc.at[0], rc.at[0], 7, x_peer)]
-    copies_b[1].wait()
-    for q in range(z_half):
-        sc[1, q] = (held(2 * (1 - y) + x, z_half + q) + rb[1, 1 - y, q].astype(F32)).astype(BF16)
-    copies_c.append(copy(sc.at[1], rc.at[1], 8, y_peer))
-    for q in range(z_half):
-        add(grp_index, q, rb[0, x, q])
-        add(grp_index, z_half + q, rb[1, y, q])
-    small_b.wait()
-    rs[2] = rs[1] + rr[1]
-    small_c = copy(rs.at[2], rr.at[2], 9, x_peer)
-    for s in range(2):
-        copies_c[s].wait()
-        for q in range(z_half):
-            add(grp_index, s * z_half + q, rc[s, q])
-    copies_d = []
-    for k in range(1, n_z):
-        sd[k - 1] = held(grp_index, lax.rem(z + k, n_z)).astype(BF16)
-        copies_d.append(copy(sd.at[k - 1], rd.at[k - 1], 9 + k, z_peers[k - 1]))
-    small_c.wait()
-    rz[z] = rs[2] + rr[2]
-    small_d = []
-    for k in range(1, n_z):
-        small_d.append(copy(rz.at[z], rz.at[z], 8 + n_z + k, z_peers[k - 1]))
+    rx[grp_index] = rs[0] + rr[0]
+    small_b = [
+        copy(rx.at[grp_index], rx.at[grp_index], 3 + k, grp_peers[k - 1]) for k in range(1, n_grp)
+    ]
+    offsets = [(dg, dz) for dz in (2, 1, 3, 0) for dg in (3, 2, 1, 0) if dg or dz]
+    copies_b = []
+    for dg, dz in offsets:
+        slot = dg * n_z + dz
+        there = (lax.rem(grp_index + dg, n_grp), lax.rem(z + dz, n_z))
+        sb[slot] = held(*there).astype(BF16)
+        copies_b.append(copy(
+            sb.at[slot], rb.at[slot], 10 + slot, (there[0], 2 * there[1] + core)
+        ))
+    for c in small_b:
+        c.wait()
+    total = rx[0]
+    for g in range(1, n_grp):
+        total = total + rx[g]
+    rz[z] = total
+    small_d = [copy(rz.at[z], rz.at[z], 6 + k, z_peers[k - 1]) for k in range(1, n_z)]
     total = held(grp_index, z)
-    for k in range(1, n_z):
-        copies_d[k - 1].wait()
-        total = total + rd[k - 1].astype(F32)
+    for (dg, dz), c in zip(offsets, copies_b):
+        c.wait()
+        total = total + rb[dg * n_z + dz].astype(F32)
     row_at = row_index * tile_rows + lax.broadcasted_iota(jnp.int32, total.shape, 0)
     col_at = grp_index * LANES + lax.broadcasted_iota(jnp.int32, total.shape, 1)
     out_ref[...] = jnp.where(row_at == col_at, 0.0, total * gram_scale)
@@ -414,21 +395,18 @@
         tile_rows = width // n_row
         n_z = n_row // 2
         tile = (tile_rows, LANES)
-        copies = 9 + 2 * n_z
+        copies = 10 + n_grp * n_z
         scratch += [
             pltpu.VMEM(gram_shape, F32),
             pltpu.VMEM(halo_shape, F32),
             pltpu.VMEM(halo_shape, F32),
             pltpu.VMEM((tiles, n_z) + tile, BF16),
             pltpu.VMEM((tiles, n_z) + tile, BF16),
-            pltpu.VMEM((2, 2, n_z // 2) + tile, BF16),
-            pltpu.VMEM((2, 2, n_z // 2) + tile, BF16),
-            pltpu.VMEM((2, n_z // 2) + tile, BF16),
-            pltpu.VMEM((2, n_z // 2) + tile, BF16),
-            pltpu.VMEM((n_z - 1,) + tile, BF16),
-            pltpu.VMEM((n_z - 1,) + tile, BF16),
-            pltpu.VMEM((3, 2 * tiles, LANES), F32),
-            pltpu.VMEM((3, 2 * tiles, LANES), F32),
+            pltpu.VMEM((n_grp * n_z,) + tile, BF16),
+            pltpu.VMEM((n_grp * n_z,) + tile, BF16),
+            pltpu.VMEM((1, 2 * tiles, LANES), F32),
+            pltpu.VMEM((1, 2 * tiles, LANES), F32),
+            pltpu.VMEM((n_grp, 2 * tiles, LANES), F32),
             pltpu.VMEM((n_z, 2 * tiles, LANES), F32),
             pltpu.SemaphoreType.DMA((copies,)),
             pltpu.SemaphoreType.DMA((copies,)),

time: 35.8 us -> 34.1 us (0.953)
  Pallas kernels: 35 us -> 33.3 us
    pallas_call x1, Pallas kernels: 32.8 us -> 31 us  [on_device(): pl.pallas_call(functools.partial(local_kernel, fused, n_grp, n_row, block...]
where the time goes in v5:
time: 34.1 us; the launch traced here: 33.9 us
  Pallas kernels  33.3 us (98%)
  between operations  0.64 us (2%)
    pallas_call x1, Pallas kernels, on_device(): pl.pallas_call(functools.partial(local_kernel, fused, n_grp, n_row, block...  31 us
    pallas_call x1, Pallas kernels, on_device(): pl.pallas_call(hand_on_kernel, out_shape=tuple((jax.ShapeDtypeStruct(r.sh...  2.25 us

profile of v5, /device:TPU:0, one launch (start us, length us, event | category | flops | bytes accessed | tf_op | source)
XLA Modules:
  0.0 33.9 jit_solution(8223792117242091775)
XLA Ops:
  0.6 31.0 %normal_equations.1 = (f32[64,128]{1,0:T(8,128)}, f32[4,128]{1,0:T(4,128)}, f32[4,128]{1,0:T(4,128)}) custom-call(f32[16,128]{1,0:T(8,128)} %bitcast.5, f32[16,128]{1,0:T(8,128)} %bitcast.6, bf16[2,2048]{1,0:T(2,128)(2,1)} %obs_in.1, bf16[2,256]{1,0:T(2,128)(2,1)} %taps_in.1, s32[16,128]{1,0:T(8,128)} %bitcast.7, s32[2,512]{1,0:T(2,128)} %har_in.1), custom_call_target="tpu_custom_call" | custom-call | tf_op jit(solution)/shard_map/normal_equations/pallas_call | solution.py:427
  31.7 2.2 %hand_on.1 = (f32[64,128]{1,0:T(8,128)}, f32[4,128]{1,0:T(4,128)}, f32[4,128]{1,0:T(4,128)}) custom-call(f32[64,128]{1,0:T(8,128)} %get-tuple-element.9.refs_0_, f32[4,128]{1,0:T(4,128)} %get-tuple-element.10.refs_1_, f32[4,128]{1,0:T(4,128)} %get-tuple-element.11.refs_2_), custom_call_target="tpu_custom_call" | custom-call | tf_op jit(solution)/shard_map/hand_on/pallas_call | solution.py:441

commit v6 on v5

--- a/solution.py
+++ b/solution.py
@@ -17,7 +17,6 @@
 COS_C = (1.41420316696167, -6.977553367614746, 5.714066982269287, -1.7246402502059937)
 TURN_HIGH = 2608.0 / 16384.0
 TURN_LOW = 1.0 / (2.0 * math.pi) - TURN_HIGH
-TURN_UNIT = 2.0**-32
 FUSED = True
 
 
@@ -39,11 +38,7 @@
 def turns(angle):
     head = nearest(angle * 1024.0) * (1.0 / 1024.0)
     tail = angle - head
-    coarse = head * TURN_HIGH
-    high = nearest(coarse * 32768.0)
-    low = (coarse - high * (1.0 / 32768.0)) + (head * TURN_LOW + tail * (TURN_HIGH + TURN_LOW))
-    fine = nearest(low * 2.0**32)
-    return high.astype(jnp.int32) * 131072 + fine.astype(jnp.int32)
+    return head * TURN_HIGH + (head * TURN_LOW + tail * (TURN_HIGH + TURN_LOW))
 
 
 def hand_on_kernel(*refs):
@@ -129,7 +124,7 @@
     degree = har_ref[0:1, :].astype(F32)
     order = har_ref[1:2, :]
     size = jnp.abs(order).astype(F32)
-    phase = jnp.where(order >= 0, 0.0, -1.0).astype(F32)
+    phase = jnp.where(order >= 0, 0.0, -0.25).astype(F32)
     turned[...] = jnp.zeros((LANES, LANES), F32)
     number = 0
     for values in (degree, size, phase):
@@ -139,10 +134,7 @@
     columns = turned[...].T
     for number in range(3):
         for t in range(col_tiles):
-            unit = 1 << 30 if number == 2 else 1
-            waves[number, t * LANES:(t + 1) * LANES, :] = (
-                spread(columns, number * col_tiles + t).astype(jnp.int32) * unit
-            )
+            waves[number, t * LANES:(t + 1) * LANES, :] = spread(columns, number * col_tiles + t)
 
     below = lax.broadcasted_iota(jnp.int32, (EXTRA, LANES), 0) == 0
 
@@ -154,8 +146,10 @@
             phi = turns(lon_ref[pl.ds(tile, 1), :])
             for chunk in range(width // CHUNK):
                 rows = slice(chunk * CHUNK, (chunk + 1) * CHUNK)
-                a = (waves[0, rows, :] * theta).astype(F32) * TURN_UNIT
-                b = (waves[1, rows, :] * phi + waves[2, rows, :]).astype(F32) * TURN_UNIT
+                a = waves[0, rows, :] * theta
+                b = waves[1, rows, :] * phi + waves[2, rows, :]
+                a = a - nearest(a)
+                b = b - nearest(b)
                 ua = a * a
                 ub = b * b
                 sin_a = a * poly(ua, SIN_C)
@@ -385,7 +379,7 @@
         pltpu.VMEM((2, 2 * taps_n, taps_n), BF16),
         pltpu.VMEM((window, LANES), F32),
         pltpu.VMEM((window // LANES, LANES), F32),
-        pltpu.VMEM((3, width, LANES), jnp.int32),
+        pltpu.VMEM((3, width, LANES), F32),
         pltpu.VMEM((LANES, LANES), F32),
     ]
     gram_shape = (tiles, width + EXTRA, LANES)

time: 34.1 us -> 34.2 us (level)
  no operation moved by 1% of the time
where the time goes in v6:
time: 34.2 us; the launch traced here: 34 us
  Pallas kernels  33.4 us (98%)
  between operations  0.64 us (2%)
    pallas_call x1, Pallas kernels, on_device(): pl.pallas_call(functools.partial(local_kernel, fused, n_grp, n_row, block...  31.2 us
    pallas_call x1, Pallas kernels, on_device(): pl.pallas_call(hand_on_kernel, out_shape=tuple((jax.ShapeDtypeStruct(r.sh...  2.25 us

profile of v6, /device:TPU:0, one launch (start us, length us, event | category | flops | bytes accessed | tf_op | source)
XLA Modules:
  0.0 34.0 jit_solution(11733603449543257083)
XLA Ops:
  0.6 31.2 %normal_equations.1 = (f32[64,128]{1,0:T(8,128)}, f32[4,128]{1,0:T(4,128)}, f32[4,128]{1,0:T(4,128)}) custom-call(f32[16,128]{1,0:T(8,128)} %bitcast.5, f32[16,128]{1,0:T(8,128)} %bitcast.6, bf16[2,2048]{1,0:T(2,128)(2,1)} %obs_in.1, bf16[2,256]{1,0:T(2,128)(2,1)} %taps_in.1, s32[16,128]{1,0:T(8,128)} %bitcast.7, s32[2,512]{1,0:T(2,128)} %har_in.1), custom_call_target="tpu_custom_call" | custom-call | tf_op jit(solution)/shard_map/normal_equations/pallas_call | solution.py:421
  31.8 2.2 %hand_on.1 = (f32[64,128]{1,0:T(8,128)}, f32[4,128]{1,0:T(4,128)}, f32[4,128]{1,0:T(4,128)}) custom-call(f32[64,128]{1,0:T(8,128)} %get-tuple-element.9.refs_0_, f32[4,128]{1,0:T(4,128)} %get-tuple-element.10.refs_1_, f32[4,128]{1,0:T(4,128)} %get-tuple-element.11.refs_2_), custom_call_target="tpu_custom_call" | custom-call | tf_op jit(solution)/shard_map/hand_on/pallas_call | solution.py:435

commit v7 on v5

--- a/solution.py
+++ b/solution.py
@@ -63,11 +63,11 @@
 ):
     if fused:
         (out_ref, right_ref, diag_ref, col_ref, lon_ref, obs_got, taps_ref, seg_ref, har_ref, in_sem,
-         obs_ref, fresh, window, filt, table, matrix, lab_col, lab, waves, turned, gram,
+         obs_ref, fresh, window, filt, filt_next, table, matrix, lab_col, lab, waves, turned, gram,
          halo_send, halo, sa, ra, sb, rb, rs, rr, rx, rz, send_sem, recv_sem) = refs
     else:
         (halo, gram, small_ref, col_ref, lon_ref, obs_got, taps_ref, seg_ref, har_ref, in_sem,
-         obs_ref, fresh, window, filt, table, matrix, lab_col, lab, waves, turned) = refs
+         obs_ref, fresh, window, filt, filt_next, table, matrix, lab_col, lab, waves, turned) = refs
     per = taps_n // LANES
     own = blocks * per
     col_tiles = width // LANES
@@ -234,6 +234,7 @@
     half_width = width // 2
     half_tiles = half_width // LANES
     gram[...] = jnp.zeros(gram.shape, F32)
+    filt[...] = jnp.zeros(filt.shape, BF16)
 
     def filter_block(block):
         slots = (lax.rem(block + blocks, blocks + 1), block)
@@ -248,7 +249,7 @@
                 for c in range(2):
                     matrix[c, at, lanes] = jnp.where(same, table[c, at, lanes], 0.0).astype(BF16)
         for c in range(2):
-            filt[:, c * taps_n:(c + 1) * taps_n] = jnp.dot(
+            filt_next[:, c * taps_n:(c + 1) * taps_n] = jnp.dot(
                 window[c], matrix[c], preferred_element_type=F32
             ).astype(BF16)
 
@@ -264,13 +265,17 @@
     @pl.loop(0, blocks - 1)
     def _(step):
         block = blocks - 1 - step
-        design_block(lax.rem(block - 2 + blocks + 1, blocks + 1))
-        filter_block(block)
         gram_half(0)
         gram_half(1)
+        filter_block(block)
+        design_block(lax.rem(block - 2 + blocks + 1, blocks + 1))
         shift()
-
+        filt[...] = filt_next[...]
+
+    gram_half(0)
+    gram_half(1)
     filter_block(0)
+    filt[...] = filt_next[...]
     copies_a = []
     for half in range(2):
         gram_half(half)
@@ -381,6 +386,7 @@
         pltpu.VMEM((2, width + EXTRA, taps_n), BF16),
         pltpu.VMEM((2, width + EXTRA, 2 * taps_n), BF16),
         pltpu.VMEM((width + EXTRA, 2 * taps_n), BF16),
+        pltpu.VMEM((width + EXTRA, 2 * taps_n), BF16),
         pltpu.VMEM((2, 2 * taps_n, taps_n), F32),
         pltpu.VMEM((2, 2 * taps_n, taps_n), BF16),
         pltpu.VMEM((window, LANES), F32),

time: 34.1 us -> 34 us (level)
  no operation moved by 1% of the time
where the time goes in v7:
time: 34 us; the launch traced here: 33.8 us
  Pallas kernels  33.1 us (97%)
  between operations  0.64 us (2%)
    pallas_call x1, Pallas kernels, on_device(): pl.pallas_call(functools.partial(local_kernel, fused, n_grp, n_row, block...  30.9 us
    pallas_call x1, Pallas kernels, on_device(): pl.pallas_call(hand_on_kernel, out_shape=tuple((jax.ShapeDtypeStruct(r.sh...  2.25 us

profile of v7, /device:TPU:0, one launch (start us, length us, event | category | flops | bytes accessed | tf_op | source)
XLA Modules:
  0.0 33.8 jit_solution(16166211158477849831)
XLA Ops:
  0.6 30.9 %normal_equations.1 = (f32[64,128]{1,0:T(8,128)}, f32[4,128]{1,0:T(4,128)}, f32[4,128]{1,0:T(4,128)}) custom-call(f32[16,128]{1,0:T(8,128)} %bitcast.5, f32[16,128]{1,0:T(8,128)} %bitcast.6, bf16[2,2048]{1,0:T(2,128)(2,1)} %obs_in.1, bf16[2,256]{1,0:T(2,128)(2,1)} %taps_in.1, s32[16,128]{1,0:T(8,128)} %bitcast.7, s32[2,512]{1,0:T(2,128)} %har_in.1), custom_call_target="tpu_custom_call" | custom-call | tf_op jit(solution)/shard_map/normal_equations/pallas_call | solution.py:433
  31.5 2.2 %hand_on.1 = (f32[64,128]{1,0:T(8,128)}, f32[4,128]{1,0:T(4,128)}, f32[4,128]{1,0:T(4,128)}) custom-call(f32[64,128]{1,0:T(8,128)} %get-tuple-element.9.refs_0_, f32[4,128]{1,0:T(4,128)} %get-tuple-element.10.refs_1_, f32[4,128]{1,0:T(4,128)} %get-tuple-element.11.refs_2_), custom_call_target="tpu_custom_call" | custom-call | tf_op jit(solution)/shard_map/hand_on/pallas_call | solution.py:447

commit v8 on v7

--- a/solution.py
+++ b/solution.py
@@ -93,10 +93,7 @@
         z_peers = [(grp_index, lax.rem(row_index + 2 * k, n_row)) for k in range(1, n_z)]
         after = (grp_index, lax.rem(row_index + 1, n_row))
         before = (grp_index, lax.rem(row_index + n_row - 1, n_row))
-        greeted = [twin, after, before] + [
-            (lax.rem(grp_index + dg, n_grp), lax.rem(row_index + 2 * dz, n_row))
-            for dg in range(n_grp) for dz in range(n_z) if dg or dz
-        ]
+        greeted = [twin, after, before] + grp_peers + z_peers
         barrier = pltpu.get_barrier_semaphore()
         for peer in greeted:
             pl.semaphore_signal(barrier, inc=1, device_id=peer, device_id_type=pl.DeviceIdType.MESH)
@@ -326,15 +323,25 @@
     small_b = [
         copy(rx.at[grp_index], rx.at[grp_index], 3 + k, grp_peers[k - 1]) for k in range(1, n_grp)
     ]
-    offsets = [(dg, dz) for dz in (2, 1, 3, 0) for dg in (3, 2, 1, 0) if dg or dz]
-    copies_b = []
-    for dg, dz in offsets:
-        slot = dg * n_z + dz
-        there = (lax.rem(grp_index + dg, n_grp), lax.rem(z + dz, n_z))
-        sb[slot] = held(*there).astype(BF16)
-        copies_b.append(copy(
-            sb.at[slot], rb.at[slot], 10 + slot, (there[0], 2 * there[1] + core)
-        ))
+    order = [2, 1, 3, 0]
+    across = {}
+    for dz in order:
+        for dg in range(1, n_grp):
+            slot = dg * n_z + dz
+            sb[slot] = held(lax.rem(grp_index + dg, n_grp), lax.rem(z + dz, n_z)).astype(BF16)
+            across[slot] = copy(sb.at[slot], rb.at[slot], 10 + slot, grp_peers[dg - 1])
+
+    def arc_sum(dz):
+        total = held(grp_index, lax.rem(z + dz, n_z))
+        for dg in range(1, n_grp):
+            across[dg * n_z + dz].wait()
+            total = total + rb[dg * n_z + dz].astype(F32)
+        return total
+
+    along = []
+    for dz in order[:-1]:
+        sb[dz] = arc_sum(dz).astype(BF16)
+        along.append(copy(sb.at[dz], rb.at[dz], 10 + dz, z_peers[dz - 1]))
     for c in small_b:
         c.wait()
     total = rx[0]
@@ -342,10 +349,10 @@
         total = total + rx[g]
     rz[z] = total
     small_d = [copy(rz.at[z], rz.at[z], 6 + k, z_peers[k - 1]) for k in range(1, n_z)]
-    total = held(grp_index, z)
-    for (dg, dz), c in zip(offsets, copies_b):
+    total = arc_sum(0)
+    for dz, c in zip(order[:-1], along):
         c.wait()
-        total = total + rb[dg * n_z + dz].astype(F32)
+        total = total + rb[dz].astype(F32)
     row_at = row_index * tile_rows + lax.broadcasted_iota(jnp.int32, total.shape, 0)
     col_at = grp_index * LANES + lax.broadcasted_iota(jnp.int32, total.shape, 1)
     out_ref[...] = jnp.where(row_at == col_at, 0.0, total * gram_scale)

time: 34 us -> 33.9 us (level)
  no operation moved by 1% of the time
where the time goes in v8:
time: 33.9 us; the launch traced here: 33.7 us
  Pallas kernels  33.1 us (98%)
  between operations  0.64 us (2%)
    pallas_call x1, Pallas kernels, on_device(): pl.pallas_call(functools.partial(local_kernel, fused, n_grp, n_row, block...  30.8 us
    pallas_call x1, Pallas kernels, on_device(): pl.pallas_call(hand_on_kernel, out_shape=tuple((jax.ShapeDtypeStruct(r.sh...  2.25 us

profile of v8, /device:TPU:0, one launch (start us, length us, event | category | flops | bytes accessed | tf_op | source)
XLA Modules:
  0.0 33.7 jit_solution(5881104130247559941)
XLA Ops:
  0.6 30.8 %normal_equations.1 = (f32[64,128]{1,0:T(8,128)}, f32[4,128]{1,0:T(4,128)}, f32[4,128]{1,0:T(4,128)}) custom-call(f32[16,128]{1,0:T(8,128)} %bitcast.5, f32[16,128]{1,0:T(8,128)} %bitcast.6, bf16[2,2048]{1,0:T(2,128)(2,1)} %obs_in.1, bf16[2,256]{1,0:T(2,128)(2,1)} %taps_in.1, s32[16,128]{1,0:T(8,128)} %bitcast.7, s32[2,512]{1,0:T(2,128)} %har_in.1), custom_call_target="tpu_custom_call" | custom-call | tf_op jit(solution)/shard_map/normal_equations/pallas_call | solution.py:440
  31.5 2.2 %hand_on.1 = (f32[64,128]{1,0:T(8,128)}, f32[4,128]{1,0:T(4,128)}, f32[4,128]{1,0:T(4,128)}) custom-call(f32[64,128]{1,0:T(8,128)} %get-tuple-element.9.refs_0_, f32[4,128]{1,0:T(4,128)} %get-tuple-element.10.refs_1_, f32[4,128]{1,0:T(4,128)} %get-tuple-element.11.refs_2_), custom_call_target="tpu_custom_call" | custom-call | tf_op jit(solution)/shard_map/hand_on/pallas_call | solution.py:454
